TPU v7x, 32 devices: a whole 2x2x4 slice. The times are simulated.
32 devices in a mesh: section: 2 (over x), mp: 2 (over y), dp: 8 (over z, core).
Axes of the slice: x: 2, y: 2, z: 4, core: 2. Of those that a mesh axis runs over, the one named last changes fastest.
Arguments:
- atoms_in: bfloat16 [64, 1280, 128], P('dp', 'mp'), may hold values from -6 to 6
- atom_token: int32 [1280], replicated, may hold values from 0 to 159, never falling along the last dimension, each value on 1 to 24 neighbouring positions
- window_start: int32 [40], P('mp'), may hold values from 0 to 1152, as said below
- noise_level: int32 [64], P('dp'), may hold values from 0 to 15
- level_table: bfloat16 [16, 384], replicated, may hold values from -6 to 6
- single_trunk: bfloat16 [160, 384], replicated, may hold values from -6 to 6
- pair: bfloat16 [160, 160, 128], replicated, may hold values from -6 to 6
- atom_gain: bfloat16 [128], replicated, may hold values from 0.5 to 1.5
- atom_qkv: bfloat16 [128, 3, 128], replicated, may hold values from -0.5 to 0.5
- atom_out: bfloat16 [128, 128], replicated, may hold values from -1 to 1
- atom_agg: bfloat16 [128, 768], replicated, may hold values from -0.5 to 0.5
- cond_weight: bfloat16 [2, 384, 3, 768], replicated, may hold values from -0.3125 to 0.3125
- cond_bias: bfloat16 [2, 3, 768], replicated, may hold values from -3 to 3
- pair_weight: bfloat16 [128, 16], P(None, 'mp'), may hold values from -0.5 to 0.5
- attn_in: bfloat16 [768, 4, 768], P(None, None, 'mp'), may hold values from -0.21875 to 0.21875
- attn_out: bfloat16 [768, 768], P('mp'), may hold values from -0.875 to 0.875
- mlp_up: bfloat16 [768, 2, 1536], P(None, None, 'mp'), may hold values from -0.21875 to 0.21875
- mlp_down: bfloat16 [1536, 768], P('mp'), may hold values from -0.15625 to 0.15625
- cotangent: bfloat16 [64, 160, 768], P('dp'), may hold values from -6 to 6
Outputs:
- token_out: bfloat16 [8, 2, 4, 160, 768], P('dp', 'section')
- atoms_grad: float32 [8, 2, 4, 1280, 128], P('dp', 'section', None, 'mp')
- atom_gain_grad: float32 [128], P('section')
- atom_qkv_grad: float32 [128, 3, 128], P('section')
- atom_out_grad: float32 [128, 128], P('section')
- atom_agg_grad: float32 [128, 768], P('section')
- cond_weight_grad: float32 [2, 384, 3, 768], P('section')
- cond_bias_grad: float32 [2, 3, 768], P('section')
- pair_weight_grad: float32 [128, 16], P('section', 'mp')
- attn_in_grad: float32 [768, 4, 768], P('section', None, 'mp')
- attn_out_grad: float32 [768, 768], P('mp', 'section')
- mlp_up_grad: float32 [768, 2, 1536], P('section', None, 'mp')
- mlp_down_grad: float32 [1536, 768], P('mp', 'section')
Inputs may be any that keep to these rules, and one draw needn't show every extreme that they name: `atom_token`: the atoms of one token are consecutive; each token has 1 to 24 atoms, some token exactly that many. `window_start`: window w starts between 32 * w - 64 and 32 * w + 32 - 128 // 2, limited to the atoms.
All inputs are finite; a program needn't handle non-finite values.
Results may differ from a plain program's by a relative error of at most 0.025.
Values may be sent and summed in bfloat16 or wider, within the bound.
A program may use at most 384 MiB of HBM per device.

v0:
```python
import jax
import jax.numpy as jnp
from jax import lax
from jax.sharding import PartitionSpec as P

CA = 128
ATOM_HEADS = 4
D = 768
QBLOCK = 32
KWIN = 128
NTOK = 160
LEVELS = 16
MICRO = 2


EPS = 1e-05
HIGH = lax.Precision.HIGHEST


def padded(array, sides, width):
    for axis, dim in sides:
        size, length = (lax.axis_size(axis), array.shape[dim])
        up = [(i, (i + 1) % size) for i in range(size - 1)]
        down = [(j, i) for i, j in up]
        last = lax.slice_in_dim(array, length - width, length, axis=dim)
        leading = lax.slice_in_dim(array, 0, width, axis=dim)
        before = lax.ppermute(last, axis, up)
        after = lax.ppermute(leading, axis, down)
        array = jnp.concatenate([before, array, after], axis=dim)
    return array


def from_partner(array, axis, apart):
    return lax.ppermute(array, axis, [(i, i ^ 1 << apart) for i in range(lax.axis_size(axis))])


def layer_norm(values):
    center = values - jnp.mean(values, -1, keepdims=True)
    inverse = lax.rsqrt(jnp.mean(center * center, -1, keepdims=True) + EPS)
    return (center * inverse, inverse)


def norm_back(normed, inverse, grad):
    return inverse * (
        grad
        - jnp.mean(grad, -1, keepdims=True)
        - normed * jnp.mean(grad * normed, -1, keepdims=True)
    )


def silu_slope(values):
    sigma = jax.nn.sigmoid(values)
    return sigma * (1.0 + values * (1.0 - sigma))


def softmax_back(attend, grad):
    return attend * (grad - jnp.sum(attend * grad, -1, keepdims=True))


def pick_state(flag, first, second):
    return jax.tree.map(lambda left, right: jnp.where(flag, left, right), first, second)


def local(
    atoms_in,
    atom_token,
    window_start,
    noise_level,
    level_table,
    single_trunk,
    pair,
    atom_gain,
    atom_qkv,
    atom_out,
    atom_agg,
    cond_weight,
    cond_bias,
    pair_weight,
    attn_in,
    attn_out,
    mlp_up,
    mlp_down,
    cotangent,
):
    low_type = jnp.bfloat16
    wide_type = jnp.float32
    section_index = lax.axis_index("section")
    is_atom = section_index == 0
    local_atoms = atoms_in.shape[1]
    batch = atoms_in.shape[0] // MICRO
    local_heads = pair_weight.shape[1]
    local_width = attn_in.shape[2]
    head_size = local_width // local_heads
    atom_size = CA // ATOM_HEADS
    local_windows = window_start.shape[0]
    half = KWIN // 2
    atom_base = lax.axis_index("mp") * local_atoms
    token_ids = jnp.arange(NTOK, dtype=jnp.int32)
    counts = jnp.sum((atom_token[:, None] == token_ids[None, :]).astype(wide_type), 0)
    own_tokens = lax.dynamic_slice_in_dim(atom_token, atom_base, local_atoms, 0)
    member = (own_tokens[:, None] == token_ids[None, :]).astype(wide_type)
    rows = (window_start - atom_base + half)[:, None] + jnp.arange(KWIN, dtype=jnp.int32)[None, :]
    gain = atom_gain.astype(wide_type)
    atom_scale = atom_size ** (-0.5)
    head_scale = head_size ** (-0.5)
    pair_normed, pair_inverse = layer_norm(pair.astype(wide_type))
    pair_low = pair_normed.astype(low_type)
    bias = jnp.einsum("ijc,ch->hij", pair_low, pair_weight, preferred_element_type=wide_type)
    level_pick = (noise_level[:, None] == jnp.arange(LEVELS, dtype=jnp.int32)[None, :]).astype(
        low_type
    )
    level_rows = jnp.dot(level_pick, level_table, preferred_element_type=wide_type)
    single = single_trunk.astype(wide_type)[None] + level_rows[:, None, :]
    single_low = layer_norm(single)[0].astype(low_type)

    def atom_front(inputs):
        wide = inputs.astype(wide_type)
        normed, inverse = layer_norm(wide)
        hidden = (normed * gain).astype(low_type)
        projected = jnp.einsum(
            "bac,ckd->bakd", hidden, atom_qkv, preferred_element_type=wide_type
        ).astype(low_type)
        extended = padded(projected[:, :, 1:], (("mp", 1),), half)
        window_kv = extended[:, rows]
        blocks = projected[:, :, 0].reshape(batch, local_windows, QBLOCK, ATOM_HEADS, atom_size)
        keys = window_kv[:, :, :, 0].reshape(batch, local_windows, KWIN, ATOM_HEADS, atom_size)
        values = window_kv[:, :, :, 1].reshape(batch, local_windows, KWIN, ATOM_HEADS, atom_size)
        scores = (
            jnp.einsum("bwqhe,bwkhe->bwhqk", blocks, keys, preferred_element_type=wide_type)
            * atom_scale
        )
        attend = jax.nn.softmax(scores, axis=-1)
        attend_low = attend.astype(low_type)
        mixed = jnp.einsum(
            "bwhqk,bwkhe->bwqhe", attend_low, values, preferred_element_type=wide_type
        )
        mixed_low = mixed.reshape(batch, local_atoms, CA).astype(low_type)
        after = wide + jnp.einsum(
            "bac,cd->bad", mixed_low, atom_out, preferred_element_type=wide_type
        )
        after_low = after.astype(low_type)
        gate_pre = jnp.einsum("bac,cd->bad", after_low, atom_agg, preferred_element_type=wide_type)
        return (
            normed,
            inverse,
            hidden,
            blocks,
            keys,
            values,
            attend,
            attend_low,
            mixed_low,
            after_low,
            gate_pre,
        )

    def atom_tokens(start):
        front = atom_front(lax.dynamic_slice_in_dim(atoms_in, start, batch, 0))
        units = jax.nn.silu(front[10])
        partial_sums = jnp.einsum("at,bad->btd", member, units, precision=HIGH)
        summed = lax.psum(partial_sums.astype(jnp.bfloat16), "mp").astype(jnp.float32)
        return (summed / counts[None, :, None]).astype(low_type)

    def token_pass(start, incoming, state):
        tokens_in = incoming.astype(wide_type)
        cond_low = lax.dynamic_slice_in_dim(single_low, start, batch, 0)
        cond = jnp.einsum(
            "bnc,jckd->bnjkd", cond_low, cond_weight, preferred_element_type=wide_type
        ) + cond_bias.astype(wide_type)
        scale_all = jax.nn.sigmoid(cond[:, :, :, 0])
        shift_all = cond[:, :, :, 1]
        gate_all = jax.nn.sigmoid(cond[:, :, :, 2])
        normed_a, inverse_a = layer_norm(tokens_in)
        inner = (normed_a * scale_all[:, :, 0] + shift_all[:, :, 0]).astype(low_type)
        proj = jnp.einsum("bnd,dke->bnke", inner, attn_in, preferred_element_type=wide_type)
        queries = proj[:, :, 0].astype(low_type).reshape(batch, NTOK, local_heads, head_size)
        keys = proj[:, :, 1].astype(low_type).reshape(batch, NTOK, local_heads, head_size)
        values = proj[:, :, 2].astype(low_type).reshape(batch, NTOK, local_heads, head_size)
        gate_sig = jax.nn.sigmoid(proj[:, :, 3])
        scores = (
            jnp.einsum("bqhe,bkhe->bhqk", queries, keys, preferred_element_type=wide_type)
            * head_scale
            + bias[None]
        )
        log_total = jax.nn.logsumexp(scores, axis=-1, keepdims=True)
        attend_low = jnp.exp(scores - log_total).astype(low_type)
        heads_out = jnp.einsum(
            "bhqk,bkhe->bqhe", attend_low, values, preferred_element_type=wide_type
        ).reshape(batch, NTOK, local_width)
        gated = (heads_out * gate_sig).astype(low_type)
        attn = lax.psum(
            jnp.einsum("bne,ed->bnd", gated, attn_out, preferred_element_type=wide_type).astype(
                jnp.bfloat16
            ),
            "mp",
        ).astype(jnp.float32)
        middle = tokens_in + gate_all[:, :, 0] * attn
        normed_m, inverse_m = layer_norm(middle)
        inner2 = (normed_m * scale_all[:, :, 1] + shift_all[:, :, 1]).astype(low_type)
        upward = jnp.einsum("bnd,dkf->bnkf", inner2, mlp_up, preferred_element_type=wide_type)
        hidden2 = (jax.nn.silu(upward[:, :, 0]) * upward[:, :, 1]).astype(low_type)
        mlp = lax.psum(
            jnp.einsum("bnf,fd->bnd", hidden2, mlp_down, preferred_element_type=wide_type).astype(
                jnp.bfloat16
            ),
            "mp",
        ).astype(jnp.float32)
        result = (middle + gate_all[:, :, 1] * mlp).astype(low_type)
        grad_out = lax.dynamic_slice_in_dim(cotangent, start, batch, 0).astype(wide_type)
        grad_gate2 = grad_out * mlp
        grad_mlp = (grad_out * gate_all[:, :, 1]).astype(low_type)
        grad_down = jnp.einsum("bnf,bnd->fd", hidden2, grad_mlp, preferred_element_type=wide_type)
        grad_hidden2 = jnp.einsum(
            "bnd,fd->bnf", grad_mlp, mlp_down, preferred_element_type=wide_type
        )
        grad_upward = jnp.stack(
            [
                grad_hidden2 * upward[:, :, 1] * silu_slope(upward[:, :, 0]),
                grad_hidden2 * jax.nn.silu(upward[:, :, 0]),
            ],
            axis=2,
        ).astype(low_type)
        grad_up = jnp.einsum("bnd,bnkf->dkf", inner2, grad_upward, preferred_element_type=wide_type)
        grad_inner2 = lax.psum(
            jnp.einsum(
                "bnkf,dkf->bnd", grad_upward, mlp_up, preferred_element_type=wide_type
            ).astype(jnp.bfloat16),
            "mp",
        ).astype(jnp.float32)
        grad_middle = grad_out + norm_back(normed_m, inverse_m, grad_inner2 * scale_all[:, :, 1])
        grad_gate1 = grad_middle * attn
        grad_attn = (grad_middle * gate_all[:, :, 0]).astype(low_type)
        grad_wout = jnp.einsum("bne,bnd->ed", gated, grad_attn, preferred_element_type=wide_type)
        grad_gated = jnp.einsum(
            "bnd,ed->bne", grad_attn, attn_out, preferred_element_type=wide_type
        )
        grad_heads = (
            (grad_gated * gate_sig).astype(low_type).reshape(batch, NTOK, local_heads, head_size)
        )
        grad_gate_pre = (grad_gated * heads_out * gate_sig * (1.0 - gate_sig)).astype(low_type)
        attend = jnp.exp(scores - log_total)
        grad_attend = jnp.einsum(
            "bqhe,bkhe->bhqk", grad_heads, values, preferred_element_type=wide_type
        )
        grad_scores = softmax_back(attend, grad_attend).astype(low_type)
        grad_bias = jnp.sum(grad_scores.astype(wide_type), 0)
        grad_query = (
            jnp.einsum("bhqk,bkhe->bqhe", grad_scores, keys, preferred_element_type=wide_type)
            * head_scale
        ).astype(low_type)
        grad_key = (
            jnp.einsum("bhqk,bqhe->bkhe", grad_scores, queries, preferred_element_type=wide_type)
            * head_scale
        ).astype(low_type)
        grad_value = jnp.einsum(
            "bhqk,bqhe->bkhe", attend_low, grad_heads, preferred_element_type=wide_type
        ).astype(low_type)
        grad_proj = jnp.stack(
            [
                grad_query.reshape(batch, NTOK, local_width),
                grad_key.reshape(batch, NTOK, local_width),
                grad_value.reshape(batch, NTOK, local_width),
                grad_gate_pre,
            ],
            axis=2,
        )
        grad_win = jnp.einsum("bnd,bnke->dke", inner, grad_proj, preferred_element_type=wide_type)
        grad_inner = lax.psum(
            jnp.einsum(
                "bnke,dke->bnd", grad_proj, attn_in, preferred_element_type=wide_type
            ).astype(jnp.bfloat16),
            "mp",
        ).astype(jnp.float32)
        grad_tokens = grad_middle + norm_back(normed_a, inverse_a, grad_inner * scale_all[:, :, 0])
        grad_scale = (
            jnp.stack([grad_inner * normed_a, grad_inner2 * normed_m], axis=2)
            * scale_all
            * (1.0 - scale_all)
        )
        grad_shift = jnp.stack([grad_inner, grad_inner2], axis=2)
        grad_gates = jnp.stack([grad_gate1, grad_gate2], axis=2) * gate_all * (1.0 - gate_all)
        grad_cond = jnp.stack([grad_scale, grad_shift, grad_gates], axis=3).astype(low_type)
        grad_condw = jnp.einsum(
            "bnc,bnjkd->jckd", cond_low, grad_cond, preferred_element_type=wide_type
        )
        grad_condb = jnp.sum(grad_cond.astype(wide_type), axis=(0, 1))
        outgoing = grad_tokens.astype(low_type)
        placed = lax.dynamic_update_slice_in_dim(state[1], result.astype(wide_type), start, 0)
        return (
            outgoing,
            placed,
            state[2],
            state[3],
            state[4],
            state[5],
            state[6],
            state[7] + grad_condw,
            state[8] + grad_condb,
            state[9] + grad_bias,
            state[10] + grad_win,
            state[11] + grad_wout,
            state[12] + grad_up,
            state[13] + grad_down,
        )

    def atom_ahead(tick, state):
        if tick >= MICRO:
            return state
        return (atom_tokens(tick * batch),) + state[1:]

    def token_tick(tick, incoming, state):
        if tick < 1:
            return state
        return token_pass((tick - 1) * batch, incoming, state)

    state = (
        jnp.zeros((batch, NTOK, D), low_type),
        jnp.zeros(cotangent.shape, wide_type),
        jnp.zeros(atoms_in.shape, wide_type),
        jnp.zeros(atom_gain.shape, wide_type),
        jnp.zeros(atom_qkv.shape, wide_type),
        jnp.zeros(atom_out.shape, wide_type),
        jnp.zeros(atom_agg.shape, wide_type),
        jnp.zeros(cond_weight.shape, wide_type),
        jnp.zeros(cond_bias.shape, wide_type),
        jnp.zeros(bias.shape, wide_type),
        jnp.zeros(attn_in.shape, wide_type),
        jnp.zeros(attn_out.shape, wide_type),
        jnp.zeros(mlp_up.shape, wide_type),
        jnp.zeros(mlp_down.shape, wide_type),
    )
    own_start = section_index * batch
    incoming = jnp.zeros((batch, NTOK, D), low_type)
    for tick in range(MICRO + 1):
        state = pick_state(is_atom, atom_ahead(tick, state), token_tick(tick, incoming, state))
        incoming = from_partner(state[0], "section", 0)
        if tick >= 1:
            atom_start = (tick - 1) * batch
            (
                atom_normed,
                atom_inverse,
                atom_hidden,
                atom_blocks,
                atom_keys,
                atom_values,
                atom_attend,
                atom_attend_low,
                atom_mixed_low,
                atom_after_low,
                atom_gate_pre,
            ) = atom_front(lax.dynamic_slice_in_dim(atoms_in, atom_start, batch, 0))
            atom_grad_tokens = incoming.astype(wide_type) / counts[None, :, None]
            grad_units = jnp.einsum("at,btd->bad", member, atom_grad_tokens, precision=HIGH)
            grad_pre = (grad_units * silu_slope(atom_gate_pre)).astype(low_type)
            grad_agg = jnp.einsum(
                "bac,bad->cd", atom_after_low, grad_pre, preferred_element_type=wide_type
            )
            grad_after = jnp.einsum(
                "bad,cd->bac", grad_pre, atom_agg, preferred_element_type=wide_type
            )
            grad_branch = grad_after.astype(low_type)
            grad_aout = jnp.einsum(
                "bac,bad->cd", atom_mixed_low, grad_branch, preferred_element_type=wide_type
            )
            grad_mixed = jnp.einsum(
                "bad,cd->bac", grad_branch, atom_out, preferred_element_type=wide_type
            ).astype(low_type)
            grad_mixed = grad_mixed.reshape(batch, local_windows, QBLOCK, ATOM_HEADS, atom_size)
            atom_grad_attend = jnp.einsum(
                "bwqhe,bwkhe->bwhqk", grad_mixed, atom_values, preferred_element_type=wide_type
            )
            atom_grad_scores = softmax_back(atom_attend, atom_grad_attend).astype(low_type)
            grad_blocks = (
                jnp.einsum(
                    "bwhqk,bwkhe->bwqhe",
                    atom_grad_scores,
                    atom_keys,
                    preferred_element_type=wide_type,
                )
                * atom_scale
            ).astype(low_type)
            grad_keys = (
                jnp.einsum(
                    "bwhqk,bwqhe->bwkhe",
                    atom_grad_scores,
                    atom_blocks,
                    preferred_element_type=wide_type,
                )
                * atom_scale
            )
            grad_values = jnp.einsum(
                "bwhqk,bwqhe->bwkhe", atom_attend_low, grad_mixed, preferred_element_type=wide_type
            )
            window_grads = jnp.stack(
                [
                    grad_keys.reshape(batch, local_windows, KWIN, CA),
                    grad_values.reshape(batch, local_windows, KWIN, CA),
                ],
                axis=3,
            )
            grad_ext = (
                jnp.zeros((batch, local_atoms + KWIN, 2, CA), wide_type)
                .at[:, rows]
                .add(window_grads)
            )
            rims = jnp.concatenate([grad_ext[:, :half], grad_ext[:, local_atoms + half :]], axis=1)
            arrived = padded(rims.astype(jnp.bfloat16), (("mp", 1),), half).astype(rims.dtype)
            core = grad_ext[:, half : half + local_atoms]
            core = (
                core.at[:, :half]
                .add(arrived[:, :half])
                .at[:, local_atoms - half :]
                .add(arrived[:, 3 * half :])
            )
            atom_grad_proj = jnp.concatenate(
                [grad_blocks.reshape(batch, local_atoms, 1, CA), core.astype(low_type)], axis=2
            )
            grad_qkv = jnp.einsum(
                "bac,bakd->ckd", atom_hidden, atom_grad_proj, preferred_element_type=wide_type
            )
            grad_hidden = jnp.einsum(
                "bakd,ckd->bac", atom_grad_proj, atom_qkv, preferred_element_type=wide_type
            )
            grad_gain = jnp.sum(grad_hidden * atom_normed, axis=(0, 1))
            grad_input = grad_after + norm_back(atom_normed, atom_inverse, grad_hidden * gain)
            atom_placed = lax.dynamic_update_slice_in_dim(state[2], grad_input, atom_start, 0)
            state = pick_state(
                is_atom,
                (
                    state[0],
                    state[1],
                    atom_placed,
                    state[3] + grad_gain,
                    state[4] + grad_qkv,
                    state[5] + grad_aout,
                    state[6] + grad_agg,
                )
                + state[7:],
                state,
            )
    other_start = (1 - section_index) * batch
    final = (
        from_partner(
            lax.dynamic_slice_in_dim(state[1], other_start, batch, 0).astype(jnp.bfloat16),
            "section",
            0,
        ).astype(jnp.float32),
        from_partner(
            lax.dynamic_slice_in_dim(state[2], other_start, batch, 0).astype(jnp.bfloat16),
            "section",
            0,
        ).astype(jnp.float32),
    )
    token_mine = lax.dynamic_slice_in_dim(state[1], own_start, batch, 0) + final[0]
    atom_mine = lax.dynamic_slice_in_dim(state[2], own_start, batch, 0) + final[1]
    grad_pair = jnp.einsum("ijc,hij->ch", pair_low.astype(wide_type), state[9], precision=HIGH)
    atom_sums = lax.psum((state[3], state[4], state[5], state[6]), ("mp", "dp"))
    token_sums = (
        lax.psum(state[7].astype(jnp.bfloat16), "dp").astype(jnp.float32),
        lax.psum(state[8].astype(jnp.bfloat16), "dp").astype(jnp.float32),
        lax.psum(grad_pair.astype(jnp.bfloat16), "dp").astype(jnp.float32),
        lax.psum(state[10].astype(jnp.bfloat16), "dp").astype(jnp.float32),
        lax.psum(state[11].astype(jnp.bfloat16), "dp").astype(jnp.float32),
        lax.psum(state[12].astype(jnp.bfloat16), "dp").astype(jnp.float32),
        lax.psum(state[13].astype(jnp.bfloat16), "dp").astype(jnp.float32),
    )
    shares = (
        lax.psum_scatter(
            atom_sums[0].astype(jnp.bfloat16), "section", scatter_dimension=0, tiled=True
        ).astype(jnp.float32),
        lax.psum_scatter(
            atom_sums[1].astype(jnp.bfloat16), "section", scatter_dimension=0, tiled=True
        ).astype(jnp.float32),
        lax.psum_scatter(
            atom_sums[2].astype(jnp.bfloat16), "section", scatter_dimension=0, tiled=True
        ).astype(jnp.float32),
        lax.psum_scatter(
            atom_sums[3].astype(jnp.bfloat16), "section", scatter_dimension=0, tiled=True
        ).astype(jnp.float32),
        lax.psum_scatter(
            token_sums[0].astype(jnp.bfloat16), "section", scatter_dimension=0, tiled=True
        ).astype(jnp.float32),
        lax.psum_scatter(
            token_sums[1].astype(jnp.bfloat16), "section", scatter_dimension=0, tiled=True
        ).astype(jnp.float32),
        lax.psum_scatter(
            token_sums[2].astype(jnp.bfloat16), "section", scatter_dimension=0, tiled=True
        ).astype(jnp.float32),
        lax.psum_scatter(
            token_sums[3].astype(jnp.bfloat16), "section", scatter_dimension=0, tiled=True
        ).astype(jnp.float32),
        lax.psum_scatter(
            token_sums[4].astype(jnp.bfloat16), "section", scatter_dimension=1, tiled=True
        ).astype(jnp.float32),
        lax.psum_scatter(
            token_sums[5].astype(jnp.bfloat16), "section", scatter_dimension=0, tiled=True
        ).astype(jnp.float32),
        lax.psum_scatter(
            token_sums[6].astype(jnp.bfloat16), "section", scatter_dimension=1, tiled=True
        ).astype(jnp.float32),
    )
    token_out = token_mine.astype(low_type).reshape(1, 1, batch, NTOK, D)
    atoms_grad = atom_mine.reshape(1, 1, batch, local_atoms, CA)
    return (
        token_out,
        atoms_grad,
        shares[0],
        shares[1],
        shares[2],
        shares[3],
        shares[4],
        shares[5],
        shares[6],
        shares[7],
        shares[8],
        shares[9],
        shares[10],
    )


def solution(mesh):
    in_specs = (
        P("dp", "mp", None),
        P(),
        P("mp"),
        P("dp"),
        P(),
        P(),
        P(),
        P(),
        P(),
        P(),
        P(),
        P(),
        P(),
        P(None, "mp"),
        P(None, None, "mp"),
        P("mp", None),
        P(None, None, "mp"),
        P("mp", None),
        P("dp", None, None),
    )
    out_specs = (
        P("dp", "section", None, None, None),
        P("dp", "section", None, "mp", None),
        P("section"),
        P("section", None, None),
        P("section", None),
        P("section", None),
        P("section", None, None, None),
        P("section", None, None),
        P("section", "mp"),
        P("section", None, "mp"),
        P("mp", "section"),
        P("section", None, "mp"),
        P("mp", "section"),
    )
    return jax.shard_map(local, mesh=mesh, in_specs=in_specs, out_specs=out_specs, check_vma=False)
```

profile of v0, /device:TPU:0, one launch (start us, length us, event | category | flops | bytes accessed | tf_op | source)
XLA Modules:
  0.0 1590.1 jit_solution(1981354650981632121)
XLA Ops:
  40.5 11.6 fusion.4
  52.2 10.5 fusion.159
  101.6 12.3 gather_fusion
  113.8 21.3 %copy.455 = bf16[20,128,4,2,128]{1,4,0,2,3:T(8,128)(2,1)} copy(bf16[20,128,4,2,128]{4,2,3,1,0:T(4,128)(2,1)} %bitcast.753) | data formatting | bytes 10485760 | tf_op jit(solution)/shard_map/gather | solution.py:124
  142.2 7.9 fusion.356
  180.2 8.7 fusion.246
  188.9 33.0 %all-reduce.20.cloned.1.call-done = bf16[4,160,768]{2,1,0:T(8,128)(2,1)} async-done(((bf16[4,160,768]{2,1,0:T(8,128)(2,1)}), bf16[4,160,768]{2,1,0:T(8,128)(2,1)}) %all-reduce.20.cloned.1.call-update) | async-done | bytes 983056 | tf_op jit(solution)/shard_map/psum | solution.py:161
  229.4 12.3 gather_fusion.1
  241.7 9.4 copy.476
  258.0 7.8 fusion.355
  325.9 14.0 all-reduce.22.cloned.1.call-done
  356.7 9.3 fusion.162
  366.0 29.4 %all-reduce.24.cloned.1.call-done = bf16[4,160,768]{2,1,0:T(8,128)(2,1)} async-done(((bf16[4,160,768]{2,1,0:T(8,128)(2,1)}), bf16[4,160,768]{2,1,0:T(8,128)(2,1)}) %all-reduce.24.cloned.1.call-update) | async-done | bytes 983056 | tf_op jit(solution)/shard_map/psum | solution.py:224
  437.6 7.3 broadcast_add_fusion
  445.0 52.3 %all-reduce.34.cloned.1.call-done = (bf16[4,160,768]{2,1,0:T(8,128)(2,1)}, bf16[4,160,768]{2,1,0:T(8,128)(2,1)}) async-done(((bf16[4,160,768]{2,1,0:T(8,128)(2,1)}, bf16[4,160,768]{2,1,0:T(8,128)(2,1)}), (bf16[4,160,768]{2,1,0:T(8,128)(2,1)}, bf16[4,160,768]{2,1,0:T(8,128)(2,1)})) %all-reduce.34.cloned.1.call-update) | async-done | bytes 1966096 | tf_op jit(solution)/shard_map/psum | solution.py:161
  512.5 15.6 collective-permute-done.5
  551.6 38.5 %all-reduce.26.cloned.1.call-done = bf16[4,160,768]{2,1,0:T(8,128)(2,1)} async-done(((bf16[4,160,768]{2,1,0:T(8,128)(2,1)}), bf16[4,160,768]{2,1,0:T(8,128)(2,1)}) %all-reduce.26.cloned.1.call-update) | async-done | bytes 983056 | tf_op jit(solution)/shard_map/psum | solution.py:191
  616.7 28.9 %all-reduce.28.cloned.1.call-done = bf16[4,160,768]{2,1,0:T(8,128)(2,1)} async-done(((bf16[4,160,768]{2,1,0:T(8,128)(2,1)}), bf16[4,160,768]{2,1,0:T(8,128)(2,1)}) %all-reduce.28.cloned.1.call-update) | async-done | bytes 983056 | tf_op jit(solution)/shard_map/psum | solution.py:224
  699.3 12.9 fusion.217
  719.2 8.5 fusion.7
  775.9 12.3 copy.508
  788.9 188.7 %scatter_fusion = f32[4,768,2,128]{3,0,2,1:T(4,128)S(1)} fusion(f32[4,768,2,128]{3,0,2,1:T(4,128)S(1)} %broadcast.548.clone, s32[2560]{0:T(1024)S(1)} %copy-done.169, f32[2560,4,2,128]{3,1,2,0:T(4,128)} %bitcast.739), kind=kCustom, calls=%fused_computation.2 | custom fusion | flops 2621440 | bytes 31467520 | tf_op jit(solution)/shard_map/scatter-add | solution.py:404
  1048.8 7.3 fusion.12
  1056.4 9.6 collective-permute-done.9
  1066.0 9.4 fusion.6
  1109.9 12.3 copy.529
  1122.6 188.7 %scatter_fusion.1 = f32[4,768,2,128]{3,0,2,1:T(4,128)S(1)} fusion(f32[4,768,2,128]{3,0,2,1:T(4,128)S(1)} %broadcast.548.clone.1, s32[2560]{0:T(1024)S(1)} %copy-done.169, f32[2560,4,2,128]{3,1,2,0:T(4,128)} %bitcast.738), kind=kCustom, calls=%fused_computation.3 | custom fusion | flops 2621440 | bytes 31467520 | tf_op jit(solution)/shard_map/scatter-add | solution.py:404
  1347.5 70.5 %all-reduce.35 = (bf16[128]{0:T(256)(128)(2,1)S(1)}, bf16[128,3,128]{2,0,1:T(8,128)(2,1)}, bf16[128,128]{1,0:T(8,128)(2,1)}, bf16[128,768]{1,0:T(8,128)(2,1)}) all-reduce(f32[128]{0:T(128)S(1)} %broadcast_select_fusion, f32[128,3,128]{2,0,1:T(8,128)} %fusion.209, ...), channel_id=1, replica_groups=mesh['section'=2,'mp'=2,'dp'=8] {'mp','dp'}, use_global_device_ids=true, to_apply=%region_55.56 | all-reduce | flops 163968 | bytes 983808 | tf_op jit(solution)/shard_map/psum | solution.py:457
  1442.6 16.3 %collective-permute-done.6 = bf16[4,160,768]{2,1,0:T(8,128)(2,1)} collective-permute-done((bf16[4,160,768]{2,1,0:T(8,128)(2,1)}, bf16[4,160,768]{2,1,0:T(8,128)(2,1)}, u32[]{:S(2)}, u32[]{:S(2)}) %collective-permute-start.6) | collective-permute-done | bytes 983072 | tf_op jit(solution)/shard_map/ppermute | solution.py:34
  1461.3 9.6 all-reduce.9
  1471.6 17.8 %all-reduce.5 = (bf16[1,3,768]{2,1,0:T(4,128)(2,1)S(1)}, bf16[64,8]{0,1:T(8,128)(2,1)S(1)}) all-reduce(bf16[1,3,768]{2,1,0:T(4,128)(2,1)S(1)} %constant_dynamic-slice_fusion, bf16[64,8]{0,1:T(8,128)(2,1)S(1)} %copy.620), channel_id=1, replica_groups=mesh['section'=2,'mp'=2,'dp'=8] {'dp'}, use_global_device_ids=true, to_apply=%region_67.68 | all-reduce | flops 2816 | bytes 11264 | tf_op jit(solution)/shard_map/psum | solution.py:460
  1497.8 74.5 %all-reduce.30.cloned.1.call-done = (bf16[1,384,3,768]{1,3,2,0:T(8,128)(2,1)}, bf16[384,4,384]{2,0,1:T(8,128)(2,1)}, bf16[384,2,768]{2,0,1:T(8,128)(2,1)}, bf16[384,384]{1,0:T(8,128)(2,1)}, bf16[768,384]{1,0:T(8,128)(2,1)}) async-done(((bf16[1,384,3,768]{1,3,2,0:T(8,128)(2,1)}, bf16[384,4,384]{2,0,1:T(8,128)(2,1)}, bf16[384,2,768]{2,0,1:T(8,128)(2,1)}, bf16[384,384]{1,0:T(8,128)(2,1)}, ...) | async-done | bytes 5013520 | tf_op jit(solution)/shard_map/psum | solution.py:459
  (792 shorter events, 603.8 us)
Async XLA Ops:
  7.2 214.7 %all-reduce.20.cloned.1.call-start = ((), (), s32[]{:S(2)}) async-start(), calls=%async_computation.9 | async-start | bytes 1966080 | tf_op jit(solution)/shard_map/psum | solution.py:161
  13.9 83.8 %collective-permute-start = (bf16[4,64,2,128]{3,1,2,0:T(8,128)(2,1)}, bf16[4,64,2,128]{3,1,2,0:T(8,128)(2,1)}, u32[]{:S(2)}, u32[]{:S(2)}) collective-permute-start(bf16[4,64,2,128]{3,1,2,0:T(8,128)(2,1)} %get-tuple-element.213), channel_id=1, source_target_pairs={{0,8},{1,9},{2,10},{3,11},{4,12},{5,13},{6,14},{7,15},{16,24},{17,... | collective-permute-start | bytes 393224 | tf_op jit(solution)/shard_map/ppermute | solution.py:27
  19.4 78.3 %collective-permute-start.1 = (bf16[4,64,2,128]{3,1,2,0:T(8,128)(2,1)}, bf16[4,64,2,128]{3,1,2,0:T(8,128)(2,1)}, u32[]{:S(2)}, u32[]{:S(2)}) collective-permute-start(bf16[4,64,2,128]{3,1,2,0:T(8,128)(2,1)} %get-tuple-element.214), channel_id=1, source_target_pairs={{8,0},{9,1},{10,2},{11,3},{12,4},{13,5},{14,6},{15,7},{24,16},{25,... | collective-permute-start | bytes 393224 | tf_op jit(solution)/shard_map/ppermute | solution.py:28
  23.3 202.6 %collective-permute-start.3 = (bf16[4,64,2,128]{3,1,2,0:T(8,128)(2,1)}, bf16[4,64,2,128]{3,1,2,0:T(8,128)(2,1)}, u32[]{:S(2)}, u32[]{:S(2)}) collective-permute-start(bf16[4,64,2,128]{3,1,2,0:T(8,128)(2,1)} %get-tuple-element.208), channel_id=1, source_target_pairs={{0,8},{1,9},{2,10},{3,11},{4,12},{5,13},{6,14},{7,15},{16,24},{17,... | collective-permute-start | bytes 393224 | tf_op jit(solution)/shard_map/ppermute | solution.py:27
  29.2 196.8 %collective-permute-start.4 = (bf16[4,64,2,128]{3,1,2,0:T(8,128)(2,1)}, bf16[4,64,2,128]{3,1,2,0:T(8,128)(2,1)}, u32[]{:S(2)}, u32[]{:S(2)}) collective-permute-start(bf16[4,64,2,128]{3,1,2,0:T(8,128)(2,1)} %get-tuple-element.209), channel_id=1, source_target_pairs={{8,0},{9,1},{10,2},{11,3},{12,4},{13,5},{14,6},{15,7},{24,16},{25,... | collective-permute-start | bytes 393224 | tf_op jit(solution)/shard_map/ppermute | solution.py:28
  97.7 124.2 %copy-start.190 = (f32[160]{0:T(256)}, f32[160]{0:T(256)S(1)}, u32[]{:S(2)}) copy-start(f32[160]{0:T(256)S(1)} %convert_reduce_fusion.9) | copy-start | bytes 1924
  180.1 159.8 %all-reduce.22.cloned.1.call-start = ((), (), s32[]{:S(2)}) async-start(), calls=%async_computation.10 | async-start | bytes 1966080 | tf_op jit(solution)/shard_map/psum | solution.py:191
  224.5 41.4 %collective-permute-start.2 = (bf16[4,160,768]{2,1,0:T(8,128)(2,1)}, bf16[4,160,768]{2,1,0:T(8,128)(2,1)}, u32[]{:S(2)}, u32[]{:S(2)}) collective-permute-start(bf16[4,160,768]{2,1,0:T(8,128)(2,1)} %fusion.222), channel_id=1, source_target_pairs={{0,16},{16,0},{1,17},{17,1},{2,18},{18,2},{3,19},{19,3},{4,20},{20... | collective-permute-start | bytes 2949128 | tf_op jit(solution)/shard_map/ppermute | solution.py:34
  302.1 93.4 %all-reduce.24.cloned.1.call-start = ((), (), s32[]{:S(2)}) async-start(), calls=%async_computation.11 | async-start | bytes 1966080 | tf_op jit(solution)/shard_map/psum | solution.py:224
  356.6 140.6 %all-reduce.34.cloned.1.call-start = ((), (), s32[]{:S(2)}) async-start(), calls=%async_computation.25 | async-start | bytes 3932160 | tf_op jit(solution)/shard_map/psum | solution.py:161
  436.9 153.2 %all-reduce.26.cloned.1.call-start = ((), (), s32[]{:S(2)}) async-start(), calls=%async_computation.12 | async-start | bytes 1966080 | tf_op jit(solution)/shard_map/psum | solution.py:191
  504.6 23.6 %collective-permute-start.5 = (bf16[4,160,768]{2,1,0:T(8,128)(2,1)S(1)}, bf16[4,160,768]{2,1,0:T(8,128)(2,1)S(1)}, u32[]{:S(2)}, u32[]{:S(2)}) collective-permute-start(bf16[4,160,768]{2,1,0:T(8,128)(2,1)S(1)} %fusion.220), channel_id=1, source_target_pairs={{0,16},{16,0},{1,17},{17,1},{2,18},{18,2},{3,19},{19,3},{4,20},{20... | collective-permute-start | bytes 2949128 | tf_op jit(solution)/shard_map/ppermute | solution.py:34
  551.4 94.3 %all-reduce.28.cloned.1.call-start = ((), (), s32[]{:S(2)}) async-start(), calls=%async_computation.13 | async-start | bytes 1966080 | tf_op jit(solution)/shard_map/psum | solution.py:224
  606.9 406.4 %all-reduce.32.cloned.1.call-start = ((), (), s32[]{:S(2)}) async-start(), calls=%async_computation.24 | async-start | bytes 5898240 | tf_op jit(solution)/shard_map/psum | solution.py:202
  681.0 738.9 %reduce-scatter.28.cloned.1.call-start = ((), (), s32[]{:S(2)}) async-start(), calls=%async_computation.20 | async-start | bytes 49152
  715.9 704.9 %reduce-scatter.30.cloned.1.call-start = ((), (), s32[]{:S(2)}) async-start(), calls=%async_computation.21 | async-start | bytes 884736
  719.1 703.5 %reduce-scatter.32.cloned.1.call-start = ((), (), s32[]{:S(2)}) async-start(), calls=%async_computation.22 | async-start | bytes 1769472
  744.8 687.8 %reduce-scatter.26.cloned.1.call-start = ((), (), s32[]{:S(2)}) async-start(), calls=%async_computation.19 | async-start | bytes 3538944 | tf_op jit(solution)/shard_map/reduce_scatter | solution.py:495
  763.9 668.6 %reduce-scatter.24.cloned.1.call-start = ((), (), s32[]{:S(2)}) async-start(), calls=%async_computation.18 | async-start | bytes 3538944 | tf_op jit(solution)/shard_map/reduce_scatter | solution.py:489
  979.0 22.2 %collective-permute-start.7 = (bf16[4,64,2,128]{3,1,2,0:T(8,128)(2,1)S(1)}, bf16[4,64,2,128]{3,1,2,0:T(8,128)(2,1)}, u32[]{:S(2)}, u32[]{:S(2)}) collective-permute-start(bf16[4,64,2,128]{3,1,2,0:T(8,128)(2,1)S(1)} %get-tuple-element.217), channel_id=1, source_target_pairs={{0,8},{1,9},{2,10},{3,11},{4,12},{5,13},{6,14},{7,15},{16,24},{17,... | collective-permute-start | bytes 393224 | tf_op jit(solution)/shard_map/ppermute | solution.py:27
  981.9 19.3 %collective-permute-start.8 = (bf16[4,64,2,128]{3,1,2,0:T(8,128)(2,1)}, bf16[4,64,2,128]{3,1,2,0:T(8,128)(2,1)}, u32[]{:S(2)}, u32[]{:S(2)}) collective-permute-start(bf16[4,64,2,128]{3,1,2,0:T(8,128)(2,1)} %get-tuple-element.218), channel_id=1, source_target_pairs={{8,0},{9,1},{10,2},{11,3},{12,4},{13,5},{14,6},{15,7},{24,16},{25,... | collective-permute-start | bytes 393224 | tf_op jit(solution)/shard_map/ppermute | solution.py:28
  1013.2 419.4 %reduce-scatter.22.cloned.1.call-start = ((), (), s32[]{:S(2)}) async-start(), calls=%async_computation.17 | async-start | bytes 5308416 | tf_op jit(solution)/shard_map/reduce_scatter | solution.py:480
  1021.1 44.9 %collective-permute-start.9 = (bf16[4,160,768]{2,1,0:T(8,128)(2,1)}, bf16[4,160,768]{2,1,0:T(8,128)(2,1)}, u32[]{:S(2)}, u32[]{:S(2)}) collective-permute-start(bf16[4,160,768]{2,1,0:T(8,128)(2,1)} %fusion.227), channel_id=1, source_target_pairs={{0,16},{16,0},{1,17},{17,1},{2,18},{18,2},{3,19},{19,3},{4,20},{20... | collective-permute-start | bytes 2949128 | tf_op jit(solution)/shard_map/ppermute | solution.py:34
  1056.2 435.0 %reduce-scatter.18.cloned.1.call-start = ((), (), s32[]{:S(2)}) async-start(), calls=%async_computation.15 | async-start | bytes 49152 | tf_op jit(solution)/shard_map/reduce_scatter | solution.py:474
  1312.6 22.6 %collective-permute-start.10 = (bf16[4,64,2,128]{3,1,2,0:T(8,128)(2,1)}, bf16[4,64,2,128]{3,1,2,0:T(8,128)(2,1)}, u32[]{:S(2)}, u32[]{:S(2)}) collective-permute-start(bf16[4,64,2,128]{3,1,2,0:T(8,128)(2,1)} %get-tuple-element.215), channel_id=1, source_target_pairs={{0,8},{1,9},{2,10},{3,11},{4,12},{5,13},{6,14},{7,15},{16,24},{17,... | collective-permute-start | bytes 393224 | tf_op jit(solution)/shard_map/ppermute | solution.py:27
  1319.0 16.2 %collective-permute-start.11 = (bf16[4,64,2,128]{3,1,2,0:T(8,128)(2,1)}, bf16[4,64,2,128]{3,1,2,0:T(8,128)(2,1)}, u32[]{:S(2)}, u32[]{:S(2)}) collective-permute-start(bf16[4,64,2,128]{3,1,2,0:T(8,128)(2,1)} %get-tuple-element.216), channel_id=1, source_target_pairs={{8,0},{9,1},{10,2},{11,3},{12,4},{13,5},{14,6},{15,7},{24,16},{25,... | collective-permute-start | bytes 393224 | tf_op jit(solution)/shard_map/ppermute | solution.py:28
  1347.5 77.4 %copy-start.90 = (bf16[4,160,2,1,768]{4,1,0,3,2:T(8,128)(2,1)S(1)}, bf16[4,160,2,1,768]{4,1,0,3,2:T(8,128)(2,1)}, u32[]{:S(2)}) copy-start(bf16[4,160,2,1,768]{4,1,0,3,2:T(8,128)(2,1)} %copy-done.89) | copy-start | bytes 5898244
  1418.1 74.4 %reduce-scatter.16.cloned.1.call-start = ((), (), s32[]{:S(2)}) async-start(), calls=%async_computation.14 | async-start | bytes 147456 | tf_op jit(solution)/shard_map/reduce_scatter | solution.py:471
  1418.7 75.3 %reduce-scatter.20.cloned.1.call-start = ((), (), s32[]{:S(2)}) async-start(), calls=%async_computation.16 | async-start | bytes 294912 | tf_op jit(solution)/shard_map/reduce_scatter | solution.py:477
  1424.8 147.6 %all-reduce.30.cloned.1.call-start = ((), (), s32[]{:S(2)}) async-start(), calls=%async_computation.23 | async-start | bytes 10027008 | tf_op jit(solution)/shard_map/psum | solution.py:459
  1430.7 28.2 %collective-permute-start.6 = (bf16[4,160,768]{2,1,0:T(8,128)(2,1)}, bf16[4,160,768]{2,1,0:T(8,128)(2,1)}, u32[]{:S(2)}, u32[]{:S(2)}) collective-permute-start(bf16[4,160,768]{2,1,0:T(8,128)(2,1)} %dynamic-slice_convert_fusion), channel_id=1, source_target_pairs={{0,16},{16,0},{1,17},{17,1},{2,18},{18,2},{3,19},{19,3},{4,20},{20... | collective-permute-start | bytes 2949128 | tf_op jit(solution)/shard_map/ppermute | solution.py:34
  1442.3 53.3 %collective-permute-start.12 = (bf16[4,640,128]{2,1,0:T(8,128)(2,1)S(1)}, bf16[4,640,128]{2,1,0:T(8,128)(2,1)}, u32[]{:S(2)}, u32[]{:S(2)}) collective-permute-start(bf16[4,640,128]{2,1,0:T(8,128)(2,1)S(1)} %dynamic-slice_convert_fusion.1), channel_id=1, source_target_pairs={{0,16},{16,0},{1,17},{17,1},{2,18},{18,2},{3,19},{19,3},{4,20},{20... | collective-permute-start | bytes 1966088 | tf_op jit(solution)/shard_map/ppermute | solution.py:34
  (232 other events, 1291.9 us)
Sparse Core Ops, SparseCore 0:
  180.2 41.6 all-reduce.19
  302.2 37.6 all-reduce.21
  356.8 38.6 all-reduce.23
  437.0 60.2 all-reduce.33
  551.5 38.6 all-reduce.25
  607.0 38.6 all-reduce.27
  681.1 81.8 all-reduce.31
  765.3 9.7 reduce-scatter.27
  778.1 15.2 reduce-scatter.29
  795.5 21.7 reduce-scatter.31
  820.2 34.6 reduce-scatter.25
  1013.3 58.1 reduce-scatter.23
  1074.4 48.1 reduce-scatter.21
  1418.2 7.3 reduce-scatter.17
  1428.2 11.0 reduce-scatter.15
  1441.4 13.1 reduce-scatter.19
  1457.8 114.4 all-reduce.29
where the time goes:
time: 1620 us; the launch traced here: 1590 us
  other arithmetic  548 us (34%)
  waiting for transfers between devices  313 us (19%)
  matrix products  292 us (18%)
  local copies, waits for them, and re-layouts  288 us (18%)
  blocking collectives  97.9 us (6%)
  starting transfers between devices  34 us (2%)
  between operations  17.7 us (1%)
    scatter-add x2, other arithmetic, local(): grad_ext = jnp.zeros((batch, local_atoms + KWIN, 2, CA), wide_type).at[:,...  377 us
    psum x2, waiting for transfers between devices, atom_tokens(): lax.psum(partial_sums.astype(jnp.bfloat16), 'mp').astype(jnp.float32)  85.3 us
    psum x1, waiting for transfers between devices, local(): lax.psum(state[7].astype(jnp.bfloat16), 'dp').astype(jnp.float32)  74.5 us
    unnamed x478, local copies, waits for them, and re-layouts  72.7 us
    psum x1, blocking collectives, local(): atom_sums = lax.psum((state[3], state[4], state[5], state[6]), ('mp', 'dp'))  70.5 us
    psum x2, waiting for transfers between devices, token_pass(): lax.psum(jnp.einsum('bnkf,dkf->bnd', grad_upward, mlp_up, preferred_eleme...  58.4 us
    gather x4, local copies, waits for them, and re-layouts, atom_front(): window_kv = extended[:, rows]  55.2 us
    psum x2, waiting for transfers between devices, token_pass(): lax.psum(jnp.einsum('bne,ed->bnd', gated, attn_out, preferred_element_typ...  52.5 us
  transfers between devices with their start and end apart: 30, of which 10 were waited for; matrix products, arithmetic and copies ran while one was open for 57% of the time, Pallas kernels for 0%

commit v1 on v0

v1 whole, which is shorter than its diff:
```python
import functools

import jax
import jax.numpy as jnp
from jax import lax
from jax.experimental import pallas as pl
from jax.experimental.pallas import tpu as pltpu
from jax.sharding import PartitionSpec as P

QBLOCK = 32
KWIN = 128
MICRO = 2
ATOM_HEADS = 4
SPAN = 2
EPS = 1e-05
LOW = jnp.bfloat16
WIDE = jnp.float32
MIB = 1 << 20


def mul(left, right):
    return lax.dot_general(left, right, (((1,), (0,)), ((), ())), preferred_element_type=WIDE)


def mul_nt(left, right):
    return lax.dot_general(left, right, (((1,), (1,)), ((), ())), preferred_element_type=WIDE)


def mul_tn(left, right):
    return lax.dot_general(left, right, (((0,), (0,)), ((), ())), preferred_element_type=WIDE)


def layer_norm(values):
    center = values - jnp.mean(values, -1, keepdims=True)
    inverse = lax.rsqrt(jnp.mean(center * center, -1, keepdims=True) + EPS)
    return center * inverse, inverse


def norm_back(normed, inverse, grad):
    return inverse * (
        grad
        - jnp.mean(grad, -1, keepdims=True)
        - normed * jnp.mean(grad * normed, -1, keepdims=True)
    )


def sigmoid(values):
    return 1.0 / (1.0 + jnp.exp(-values))


def params(mib, semantics=None):
    return pltpu.CompilerParams(vmem_limit_bytes=mib * MIB, dimension_semantics=semantics)


def cost(flops, moved, exps=0):
    return pl.CostEstimate(flops=int(flops), bytes_accessed=int(moved), transcendentals=int(exps))


def sds(shape, dtype):
    return jax.ShapeDtypeStruct(shape, dtype)


def pair_kernel(pair_ref, weight_ref, low_ref, bias_ref):
    normed, _ = layer_norm(pair_ref[...].astype(WIDE))
    low = normed.astype(LOW)
    low_ref[...] = low
    for i in range(low.shape[0]):
        bias_ref[:, i, :] = mul_nt(weight_ref[...], low[i])


def pair_bias(pair, weight):
    tokens, width = pair.shape[1], pair.shape[2]
    heads, block = weight.shape[0], 8
    return pl.pallas_call(
        pair_kernel,
        grid=(tokens // block,),
        in_specs=[
            pl.BlockSpec((block, tokens, width), lambda i: (i, 0, 0)),
            pl.BlockSpec((heads, width), lambda i: (0, 0)),
        ],
        out_specs=[
            pl.BlockSpec((block, tokens, width), lambda i: (i, 0, 0)),
            pl.BlockSpec((heads, block, tokens), lambda i: (0, i, 0)),
        ],
        out_shape=[sds(pair.shape, LOW), sds((heads, tokens, tokens), WIDE)],
        compiler_params=params(24),
        cost_estimate=cost(20e9, 16e6),
        name="pair_bias",
    )(pair, weight)


def pair_back_kernel(low_ref, grad_ref, out_ref):
    @pl.when(pl.program_id(0) == 0)
    def _():
        out_ref[...] = jnp.zeros_like(out_ref)

    total = out_ref[...]
    heads = grad_ref.shape[0]
    for i in range(low_ref.shape[0]):
        grad = grad_ref[:, i, :]
        high = grad.astype(LOW)
        rest = (grad - high.astype(WIDE)).astype(LOW)
        both = mul(jnp.concatenate([high, rest], 0), low_ref[i])
        total += both[:heads] + both[heads:]
    out_ref[...] = total


def pair_back(low, grad):
    tokens, width = low.shape[1], low.shape[2]
    heads, block = grad.shape[0], 8
    return pl.pallas_call(
        pair_back_kernel,
        grid=(tokens // block,),
        in_specs=[
            pl.BlockSpec((block, tokens, width), lambda i: (i, 0, 0)),
            pl.BlockSpec((heads, block, tokens), lambda i: (0, i, 0)),
        ],
        out_specs=pl.BlockSpec((heads, width), lambda i: (0, 0)),
        out_shape=sds((heads, width), WIDE),
        compiler_params=params(24),
        cost_estimate=cost(10e9, 9e6),
        name="pair_back",
    )(low, grad)


def cond_kernel(trunk_ref, level_ref, weight_ref, bias_ref, low_ref, cond_ref):
    step = pl.program_id(0)
    samples, tokens = level_ref.shape[0], trunk_ref.shape[0]

    @pl.when(step == 0)
    def _():
        trunk = trunk_ref[...].astype(WIDE)
        for s in range(samples):
            normed, _ = layer_norm(trunk + level_ref[s])
            low_ref[s * tokens : (s + 1) * tokens, :] = normed.astype(LOW)

    value = mul(low_ref[...], weight_ref[0]) + bias_ref[0]
    cond_ref[0] = jnp.where(step % 3 == 1, value, sigmoid(value))


def conditioning(trunk, levels, weight, bias):
    tokens, width = trunk.shape
    samples, parts, wide = levels.shape[0], weight.shape[0], weight.shape[2]
    rows = samples * tokens
    return pl.pallas_call(
        cond_kernel,
        grid=(parts,),
        in_specs=[
            pl.BlockSpec((tokens, width), lambda i: (0, 0)),
            pl.BlockSpec((samples, 1, width), lambda i: (0, 0, 0)),
            pl.BlockSpec((1, width, wide), lambda i: (i, 0, 0)),
            pl.BlockSpec((1, 1, wide), lambda i: (i, 0, 0)),
        ],
        out_specs=[
            pl.BlockSpec((rows, width), lambda i: (0, 0)),
            pl.BlockSpec((1, rows, wide), lambda i: (i, 0, 0)),
        ],
        out_shape=[sds((rows, width), LOW), sds((parts, rows, wide), WIDE)],
        compiler_params=params(24),
        cost_estimate=cost(4e9, 10e6),
        name="conditioning",
    )(trunk, levels, weight, bias)


def lane_heads(rows, width, size):
    return lax.broadcasted_iota(jnp.int32, (rows, width), 1) // size


def spread(values, heads):
    head = lane_heads(values.shape[0], values.shape[1], values.shape[1] // heads)
    zero = jnp.zeros_like(values)
    return jnp.concatenate([jnp.where(head == h, values, zero) for h in range(heads)], 0)


def gather_heads(values, heads):
    rows = values.shape[0] // heads
    head = lane_heads(rows, values.shape[1], values.shape[1] // heads)
    total = jnp.where(head == 0, values[:rows], 0.0)
    for h in range(1, heads):
        total += jnp.where(head == h, values[h * rows : (h + 1) * rows], 0.0)
    return total


def key_base(group, atoms):
    start = group * SPAN * QBLOCK - KWIN // 2
    return pl.multiple_of(jnp.clip(start, 0, atoms - KWIN - (SPAN - 1) * QBLOCK - QBLOCK), QBLOCK)


def atom_front_kernel(
    atoms_ref, gain_ref, qkv_w_ref, out_w_ref, agg_w_ref, rel_ref, ids_ref, inv_ref,
    qkv_ref, probs_ref, mixed_ref, tokens_ref,
    total,
):
    atoms, width = atoms_ref.shape[1], atoms_ref.shape[2]
    groups, keys_in = probs_ref.shape[1], probs_ref.shape[2]
    queries_in = SPAN * QBLOCK
    scale = (width // ATOM_HEADS) ** (-0.5)
    wide = atoms_ref[0].astype(WIDE)
    normed, _ = layer_norm(wide)
    hidden = (normed * gain_ref[...].astype(WIDE)).astype(LOW)
    qkv_ref[0] = mul(hidden, qkv_w_ref[...]).astype(LOW)
    place = lax.broadcasted_iota(jnp.int32, (keys_in, ATOM_HEADS * queries_in), 0)

    def attend(group, carry):
        base = key_base(group, atoms)
        first = pl.multiple_of(group * queries_in, queries_in)
        queries = spread(qkv_ref[0, pl.ds(first, queries_in), :width], ATOM_HEADS)
        keys = qkv_ref[0, pl.ds(base, keys_in), width : 2 * width]
        values = qkv_ref[0, pl.ds(base, keys_in), 2 * width :]
        offset = place - rel_ref[group]
        scores = mul_nt(keys, queries) * scale
        scores = jnp.where((offset >= 0) & (offset < KWIN), scores, -1e30)
        exps = jnp.exp(scores - jnp.max(scores, 0, keepdims=True))
        probs = (exps * (1.0 / jnp.sum(exps, 0, keepdims=True))).astype(LOW)
        probs_ref[0, group] = probs
        mixed_ref[0, pl.ds(first, queries_in), :] = gather_heads(
            mul_tn(probs, values), ATOM_HEADS
        ).astype(LOW)
        return carry

    lax.fori_loop(0, groups, attend, 0)
    chunk = 256
    ids = lax.broadcasted_iota(jnp.int32, (total.shape[0], chunk), 0)
    for i in range(atoms // chunk):
        rows = slice(i * chunk, (i + 1) * chunk)
        after = wide[rows] + mul(mixed_ref[0, rows, :], out_w_ref[...])
        pre = mul(after.astype(LOW), agg_w_ref[...])
        units = (pre * sigmoid(pre)).astype(LOW)
        member = jnp.where(ids == ids_ref[:, rows], 1.0, 0.0).astype(LOW)
        part = mul(member, units)
        if i == 0:
            total[...] = part
        else:
            total[...] += part
    tokens_ref[0] = (total[...] * inv_ref[...]).astype(LOW)


def atom_front(atoms, gain, qkv_w, out_w, agg_w, rel, ids, inverse_counts):
    samples, count, width = atoms.shape
    groups = count // (SPAN * QBLOCK)
    keys_in = KWIN + SPAN * QBLOCK
    lanes = ATOM_HEADS * SPAN * QBLOCK
    tokens, wide = inverse_counts.shape[0], agg_w.shape[1]

    def whole(array):
        return pl.BlockSpec(array.shape, lambda i: (0,) * array.ndim)

    def sample(*shape):
        return pl.BlockSpec((1,) + shape, lambda i: (i,) + (0,) * len(shape))

    return pl.pallas_call(
        atom_front_kernel,
        grid=(samples,),
        in_specs=[sample(count, width)]
        + [whole(a) for a in (gain, qkv_w, out_w, agg_w, rel, ids, inverse_counts)],
        out_specs=[
            sample(count, 3 * width),
            sample(groups, keys_in, lanes),
            sample(count, width),
            sample(tokens, wide),
        ],
        out_shape=[
            sds((samples, count, 3 * width), LOW),
            sds((samples, groups, keys_in, lanes), LOW),
            sds((samples, count, width), LOW),
            sds((samples, tokens, wide), LOW),
        ],
        scratch_shapes=[pltpu.VMEM((tokens, wide), WIDE)],
        compiler_params=params(48),
        cost_estimate=cost(20e9, 12e6),
        name="atom_front",
    )(atoms, gain, qkv_w, out_w, agg_w, rel, ids, inverse_counts)


def atom_back_kernel(
    atoms_ref, gain_ref, qkv_w_ref, out_w_ref, agg_w_ref, ids_ref, inv_ref,
    qkv_ref, probs_ref, mixed_ref, grad_ref,
    atoms_grad_ref, gain_grad_ref, qkv_grad_ref, out_grad_ref, agg_grad_ref,
    after_grad, mixed_grad, key_grad, value_grad, proj_grad,
):
    atoms, width = atoms_ref.shape[1], atoms_ref.shape[2]
    groups, keys_in = probs_ref.shape[1], probs_ref.shape[2]
    queries_in = SPAN * QBLOCK
    scale = (width // ATOM_HEADS) ** (-0.5)

    @pl.when(pl.program_id(0) == 0)
    def _():
        for ref in (gain_grad_ref, qkv_grad_ref, out_grad_ref, agg_grad_ref):
            ref[...] = jnp.zeros_like(ref)

    grad = (grad_ref[0].astype(WIDE) * inv_ref[...]).astype(LOW)
    chunk = 256
    token_ids = lax.broadcasted_iota(jnp.int32, (chunk, grad.shape[0]), 1)
    for i in range(atoms // chunk):
        rows = slice(i * chunk, (i + 1) * chunk)
        mixed = mixed_ref[0, rows, :]
        after = atoms_ref[0, rows, :].astype(WIDE) + mul(mixed, out_w_ref[...])
        after_low = after.astype(LOW)
        pre = mul(after_low, agg_w_ref[...])
        sigma = sigmoid(pre)
        member = jnp.where(token_ids == ids_ref[rows, :], 1.0, 0.0).astype(LOW)
        unit_grad = mul(member, grad)
        pre_grad = (unit_grad * (sigma * (1.0 + pre * (1.0 - sigma)))).astype(LOW)
        agg_grad_ref[...] += mul_tn(after_low, pre_grad)
        after_back = mul_nt(pre_grad, agg_w_ref[...])
        after_grad[rows, :] = after_back
        branch = after_back.astype(LOW)
        out_grad_ref[...] += mul_tn(mixed, branch)
        mixed_grad[rows, :] = mul_nt(branch, out_w_ref[...]).astype(LOW)
    key_grad[...] = jnp.zeros_like(key_grad)
    value_grad[...] = jnp.zeros_like(value_grad)

    def attend(group, carry):
        base = key_base(group, atoms)
        first = pl.multiple_of(group * queries_in, queries_in)
        queries = spread(qkv_ref[0, pl.ds(first, queries_in), :width], ATOM_HEADS)
        grads = spread(mixed_grad[pl.ds(first, queries_in), :], ATOM_HEADS)
        keys = qkv_ref[0, pl.ds(base, keys_in), width : 2 * width]
        values = qkv_ref[0, pl.ds(base, keys_in), 2 * width :]
        probs_low = probs_ref[0, group]
        probs = probs_low.astype(WIDE)
        probs_grad = mul_nt(values, grads)
        mean = jnp.sum(probs * probs_grad, 0, keepdims=True)
        scores_grad = (probs * (probs_grad - mean)).astype(LOW)
        query_grad = gather_heads(mul_tn(scores_grad, keys), ATOM_HEADS)
        proj_grad[pl.ds(first, queries_in), :width] = (query_grad * scale).astype(LOW)
        key_grad[pl.ds(base, keys_in), :] += mul(scores_grad, queries)
        value_grad[pl.ds(base, keys_in), :] += mul(probs_low, grads)
        return carry

    lax.fori_loop(0, groups, attend, 0)
    proj_grad[:, width : 2 * width] = (key_grad[...] * scale).astype(LOW)
    proj_grad[:, 2 * width :] = value_grad[...].astype(LOW)
    gain = gain_ref[...].astype(WIDE)
    normed, inverse = layer_norm(atoms_ref[0].astype(WIDE))
    hidden = (normed * gain).astype(LOW)
    proj = proj_grad[...]
    qkv_grad_ref[...] += mul_tn(hidden, proj)
    hidden_grad = mul_nt(proj, qkv_w_ref[...])
    gain_grad_ref[...] += jnp.sum(hidden_grad * normed, 0, keepdims=True)
    atoms_grad_ref[0] = after_grad[...] + norm_back(normed, inverse, hidden_grad * gain)


def atom_back(atoms, gain, qkv_w, out_w, agg_w, ids, inverse_counts, qkv, probs, mixed, grad):
    samples, count, width = atoms.shape
    wide = agg_w.shape[1]

    def whole(shape):
        return pl.BlockSpec(shape, lambda i: (0,) * len(shape))

    def sample(array):
        return pl.BlockSpec((1,) + array.shape[1:], lambda i: (i,) + (0,) * (array.ndim - 1))

    fixed = (gain, qkv_w, out_w, agg_w, ids, inverse_counts)
    return pl.pallas_call(
        atom_back_kernel,
        grid=(samples,),
        in_specs=[sample(atoms)]
        + [whole(a.shape) for a in fixed]
        + [sample(a) for a in (qkv, probs, mixed, grad)],
        out_specs=[
            sample(atoms),
            whole((1, width)),
            whole((width, 3 * width)),
            whole((width, width)),
            whole((width, wide)),
        ],
        out_shape=[
            sds(atoms.shape, WIDE),
            sds((1, width), WIDE),
            sds((width, 3 * width), WIDE),
            sds((width, width), WIDE),
            sds((width, wide), WIDE),
        ],
        scratch_shapes=[
            pltpu.VMEM((count, width), WIDE),
            pltpu.VMEM((count, width), LOW),
            pltpu.VMEM((count, width), WIDE),
            pltpu.VMEM((count, width), WIDE),
            pltpu.VMEM((count, 3 * width), LOW),
        ],
        compiler_params=params(48),
        cost_estimate=cost(40e9, 12e6),
        name="atom_back",
    )(atoms, *fixed, qkv, probs, mixed, grad)


def token_attention_kernel(
    tokens_ref, scale_ref, shift_ref, gate_ref, bias_ref, in_a_ref, in_b_ref, out_a_ref, out_b_ref,
    inner_ref, qkv_ref, sig_ref, heads_ref, gated_ref, probs_ref, attn_ref, middle_ref,
):
    rows, width = tokens_ref.shape
    samples, heads, count = probs_ref.shape[0], probs_ref.shape[1], probs_ref.shape[2]
    local = in_a_ref.shape[1] // 4
    size = 2 * local // heads
    scale = size ** (-0.5)
    wide = tokens_ref[...].astype(WIDE)
    normed, _ = layer_norm(wide)
    inner = (normed * scale_ref[0] + shift_ref[0]).astype(LOW)
    inner_ref[...] = inner
    for half, weight_ref in enumerate((in_a_ref, in_b_ref)):
        qkv_ref[half] = mul(inner, weight_ref[:, : 3 * local]).astype(LOW)
        sig_ref[half] = sigmoid(mul(inner, weight_ref[:, 3 * local :]))
        for s in range(samples):
            at = slice(s * count, (s + 1) * count)
            outs = []
            for h in range(heads // 2):
                col = h * size
                query = qkv_ref[half, at, col : col + size]
                key = qkv_ref[half, at, local + col : local + col + size]
                value = qkv_ref[half, at, 2 * local + col : 2 * local + col + size]
                scores = mul_nt(query, key) * scale + bias_ref[half * (heads // 2) + h]
                exps = jnp.exp(scores - jnp.max(scores, -1, keepdims=True))
                probs = (exps * (1.0 / jnp.sum(exps, -1, keepdims=True))).astype(LOW)
                probs_ref[s, half * (heads // 2) + h] = probs
                outs.append(mul(probs, value))
            heads_ref[half, at, :] = jnp.concatenate(outs, 1)
        gated_ref[half] = (heads_ref[half] * sig_ref[half]).astype(LOW)
    attn = mul(gated_ref[0], out_a_ref[...]) + mul(gated_ref[1], out_b_ref[...])
    attn_ref[...] = attn
    middle_ref[...] = wide + gate_ref[0] * attn


def vmem(count):
    return [pl.BlockSpec(memory_space=pltpu.VMEM)] * count


def part(index, shape):
    return pl.BlockSpec((1,) + shape, lambda i: (index,) + (0,) * len(shape))


def token_attention(tokens, cond, bias, in_a, in_b, out_a, out_b):
    rows, width = tokens.shape
    heads, count = bias.shape[0], bias.shape[1]
    samples, local = rows // count, in_a.shape[1] // 4

    def whole(shape):
        return pl.BlockSpec(shape, lambda i: (0,) * len(shape))

    outs = [
        ((rows, width), LOW),
        ((2, rows, 3 * local), LOW),
        ((2, rows, local), WIDE),
        ((2, rows, local), WIDE),
        ((2, rows, local), LOW),
        ((samples, heads, count, count), LOW),
        ((rows, width), WIDE),
        ((rows, width), WIDE),
    ]
    return pl.pallas_call(
        token_attention_kernel,
        grid=(1,),
        in_specs=[whole(tokens.shape)]
        + [part(i, (rows, width)) for i in (0, 1, 2)]
        + [whole(a.shape) for a in (bias, in_a, in_b, out_a, out_b)],
        out_specs=[whole(shape) for shape, _ in outs],
        out_shape=[sds(*out) for out in outs],
        compiler_params=params(56),
        cost_estimate=cost(40e9, 20e6),
        name="token_attention",
    )(tokens, cond, cond, cond, bias, in_a, in_b, out_a, out_b)


def transition_kernel(
    middle_ref, scale_ref, shift_ref, gate_ref, grad_ref, low_ref,
    up_a_ref, up_b_ref, down_a_ref, down_b_ref,
    result_ref, middle_grad_ref, weight_grad_ref, cond_grad_ref, cond_bias_ref,
    up_ref, hidden_ref,
):
    local = down_a_ref.shape[0]
    width = middle_ref.shape[1]
    half_rows, half_cols = width // 2, width // 2
    middle = middle_ref[...]
    normed, inverse = layer_norm(middle)
    scale = scale_ref[0]
    inner = (normed * scale + shift_ref[0]).astype(LOW)
    mlp = None
    for half, (weight_ref, down_ref) in enumerate(((up_a_ref, down_a_ref), (up_b_ref, down_b_ref))):
        up_ref[half] = mul(inner, weight_ref[...])
        gate_in = up_ref[half, :, :local]
        hidden = (gate_in * sigmoid(gate_in) * up_ref[half, :, local:]).astype(LOW)
        hidden_ref[half] = hidden
        add = mul(hidden, down_ref[...])
        mlp = add if mlp is None else mlp + add
    gate = gate_ref[0]
    result_ref[...] = (middle + gate * mlp).astype(LOW)
    grad = grad_ref[...].astype(WIDE)
    mlp_grad = (grad * gate).astype(LOW)
    inner_t = inner.T
    inner_grad = None
    for half, (weight_ref, down_ref) in enumerate(((up_a_ref, down_a_ref), (up_b_ref, down_b_ref))):
        hidden_t = hidden_ref[half].T
        for sec in range(2):
            weight_grad_ref[half, sec, 4 * half_rows :, :] = mul(
                hidden_t, mlp_grad[:, sec * half_cols : (sec + 1) * half_cols]
            ).astype(LOW)
        hidden_grad = mul_nt(mlp_grad, down_ref[...])
        gate_in = up_ref[half, :, :local]
        sigma = sigmoid(gate_in)
        first = (
            hidden_grad * up_ref[half, :, local:] * (sigma * (1.0 + gate_in * (1.0 - sigma)))
        ).astype(LOW)
        second = (hidden_grad * (gate_in * sigma)).astype(LOW)
        up_grad = jnp.concatenate([first, second], 1)
        for sec in range(2):
            rows = slice(sec * half_rows, (sec + 1) * half_rows)
            for block in range(4):
                weight_grad_ref[
                    half, sec, block * half_rows : (block + 1) * half_rows, :
                ] = mul(
                    inner_t[rows], up_grad[:, block * half_cols : (block + 1) * half_cols]
                ).astype(LOW)
        add = mul_nt(up_grad, weight_ref[...])
        inner_grad = add if inner_grad is None else inner_grad + add
    middle_grad_ref[...] = grad + norm_back(normed, inverse, inner_grad * scale)
    low_t = low_ref[...].T
    pieces = (
        inner_grad * normed * (scale * (1.0 - scale)),
        inner_grad,
        grad * mlp * (gate * (1.0 - gate)),
    )
    for k, piece in enumerate(pieces):
        piece = piece.astype(LOW)
        cond_grad_ref[k] = mul(low_t, piece).astype(LOW)
        cond_bias_ref[k] = jnp.sum(piece.astype(WIDE), 0, keepdims=True)


def transition(middle, cond, grad, low, up_a, up_b, down_a, down_b):
    rows, width = middle.shape
    local, half = down_a.shape[0], width // 2

    def whole(shape):
        return pl.BlockSpec(shape, lambda i: (0,) * len(shape))

    outs = [
        ((rows, width), LOW),
        ((rows, width), WIDE),
        ((2, 2, 4 * half + local, half), LOW),
        ((3, low.shape[1], width), LOW),
        ((3, 1, width), WIDE),
    ]
    return pl.pallas_call(
        transition_kernel,
        grid=(1,),
        in_specs=[whole(middle.shape)]
        + [part(i, (rows, width)) for i in (3, 4, 5)]
        + [whole(a.shape) for a in (grad, low, up_a, up_b, down_a, down_b)],
        out_specs=[whole(shape) for shape, _ in outs],
        out_shape=[sds(*out) for out in outs],
        scratch_shapes=[
            pltpu.VMEM((2, rows, 2 * local), WIDE),
            pltpu.VMEM((2, rows, local), LOW),
        ],
        compiler_params=params(56),
        cost_estimate=cost(60e9, 20e6),
        name="transition",
    )(middle, cond, cond, cond, grad, low, up_a, up_b, down_a, down_b)


def attention_back_kernel(
    middle_grad_ref, tokens_ref, scale_ref, gate_ref, attn_ref, low_ref, inner_ref, qkv_ref,
    sig_ref, heads_ref, gated_ref, probs_ref, in_a_ref, in_b_ref, out_a_ref, out_b_ref,
    token_grad_ref, weight_grad_ref, cond_grad_ref, cond_bias_ref, bias_grad_ref,
    proj_ref, heads_grad_ref,
):
    rows, width = tokens_ref.shape
    samples, heads, count = probs_ref.shape[0], probs_ref.shape[1], probs_ref.shape[2]
    local = in_a_ref.shape[1] // 4
    size = 2 * local // heads
    head_scale = size ** (-0.5)
    half_rows = width // 2
    middle_grad = middle_grad_ref[...]
    gate = gate_ref[0]
    attn_grad = (middle_grad * gate).astype(LOW)
    inner_t = inner_ref[...].T
    inner_grad = None
    for half, (weight_ref, out_ref) in enumerate(((in_a_ref, out_a_ref), (in_b_ref, out_b_ref))):
        gated_t = gated_ref[half].T
        for sec in range(2):
            weight_grad_ref[half, sec, 4 * half_rows :, :] = mul(
                gated_t, attn_grad[:, sec * half_rows : (sec + 1) * half_rows]
            ).astype(LOW)
        gated_grad = mul_nt(attn_grad, out_ref[...])
        sig = sig_ref[half]
        with_sig = gated_grad * sig
        heads_grad_ref[...] = with_sig.astype(LOW)
        proj_ref[:, 3 * local :] = (with_sig * heads_ref[half] * (1.0 - sig)).astype(LOW)
        for s in range(samples):
            at = slice(s * count, (s + 1) * count)
            grads = ([], [], [])
            for h in range(heads // 2):
                col, index = h * size, half * (heads // 2) + h
                query = qkv_ref[half, at, col : col + size]
                key = qkv_ref[half, at, local + col : local + col + size]
                value = qkv_ref[half, at, 2 * local + col : 2 * local + col + size]
                grad = heads_grad_ref[at, col : col + size]
                probs_low = probs_ref[s, index]
                probs = probs_low.astype(WIDE)
                probs_grad = mul_nt(grad, value)
                mean = jnp.sum(probs * probs_grad, -1, keepdims=True)
                scores_grad = (probs * (probs_grad - mean)).astype(LOW)
                if s == 0:
                    bias_grad_ref[index] = scores_grad.astype(WIDE)
                else:
                    bias_grad_ref[index] += scores_grad.astype(WIDE)
                grads[0].append(mul(scores_grad, key) * head_scale)
                grads[1].append(mul_tn(scores_grad, query) * head_scale)
                grads[2].append(mul_tn(probs_low, grad))
            for k in range(3):
                proj_ref[at, k * local : (k + 1) * local] = jnp.concatenate(grads[k], 1).astype(LOW)
        proj = proj_ref[...]
        for sec in range(2):
            for k in range(4):
                weight_grad_ref[half, sec, k * half_rows : (k + 1) * half_rows, :] = mul(
                    inner_t[sec * half_rows : (sec + 1) * half_rows],
                    proj[:, k * local : (k + 1) * local],
                ).astype(LOW)
        add = mul_nt(proj, weight_ref[...])
        inner_grad = add if inner_grad is None else inner_grad + add
    scale = scale_ref[0]
    normed, inverse = layer_norm(tokens_ref[...].astype(WIDE))
    token_grad_ref[...] = (middle_grad + norm_back(normed, inverse, inner_grad * scale)).astype(LOW)
    low_t = low_ref[...].T
    pieces = (
        inner_grad * normed * (scale * (1.0 - scale)),
        inner_grad,
        middle_grad * attn_ref[...] * (gate * (1.0 - gate)),
    )
    for k, piece in enumerate(pieces):
        piece = piece.astype(LOW)
        cond_grad_ref[k] = mul(low_t, piece).astype(LOW)
        cond_bias_ref[k] = jnp.sum(piece.astype(WIDE), 0, keepdims=True)


def attention_back(
    middle_grad, tokens, cond, attn, low, inner, qkv, sig, heads_out, gated, probs,
    in_a, in_b, out_a, out_b,
):
    rows, width = tokens.shape
    heads, count = probs.shape[1], probs.shape[2]
    local, half = in_a.shape[1] // 4, width // 2

    def whole(shape):
        return pl.BlockSpec(shape, lambda i: (0,) * len(shape))

    outs = [
        ((rows, width), LOW),
        ((2, 2, 4 * half + local, half), LOW),
        ((3, low.shape[1], width), LOW),
        ((3, 1, width), WIDE),
        ((heads, count, count), WIDE),
    ]
    after = (attn, low, inner, qkv, sig, heads_out, gated, probs, in_a, in_b, out_a, out_b)
    return pl.pallas_call(
        attention_back_kernel,
        grid=(1,),
        in_specs=[whole(middle_grad.shape), whole(tokens.shape)]
        + [part(i, (rows, width)) for i in (0, 2)]
        + [whole(a.shape) for a in after],
        out_specs=[whole(shape) for shape, _ in outs],
        out_shape=[sds(*out) for out in outs],
        scratch_shapes=[pltpu.VMEM((rows, 4 * local), LOW), pltpu.VMEM((rows, local), LOW)],
        compiler_params=params(56),
        cost_estimate=cost(60e9, 24e6),
        name="attention_back",
    )(middle_grad, tokens, cond, cond, *after)


def swap(array, axis, bit=0):
    size = lax.axis_size(axis)
    return lax.ppermute(array, axis, [(i, i ^ (1 << bit)) for i in range(size)])


def side(axis, bit=0):
    return (lax.axis_index(axis) >> bit) & 1


def sum_half(array, axis, bit, dim):
    size, me = array.shape[dim] // 2, side(axis, bit)
    other = lax.dynamic_slice_in_dim(array, (1 - me) * size, size, dim)
    mine = lax.dynamic_slice_in_dim(array, me * size, size, dim)
    return (mine.astype(WIDE) + swap(other, axis, bit).astype(WIDE)).astype(array.dtype)


def both_halves(array, axis, bit, dim):
    other, me = swap(array, axis, bit), side(axis, bit)
    first, second = jnp.where(me == 0, array, other), jnp.where(me == 0, other, array)
    return jnp.concatenate([first, second], dim)


def far_bits():
    return range(1, lax.axis_size("dp").bit_length() - 1)


def sum_far(array, dim):
    for bit in far_bits():
        array = sum_half(array, "dp", bit, dim)
    for bit in reversed(far_bits()):
        array = both_halves(array, "dp", bit, dim)
    return array


def fetch(weight):
    size = weight.shape[0] // 2
    own = lax.dynamic_slice_in_dim(weight, side("dp") * size, size, 0)
    return both_halves(swap(own, "mp"), "dp", 0, 0)


def sum_split(grads):
    part = sum_half(grads, "dp", 0, 2)
    part = (part[0].astype(WIDE) + swap(part[1], "mp").astype(WIDE)).astype(LOW)
    part = sum_half(part, "section", 0, 0)[0]
    return both_halves(sum_far(part, 0), "dp", 0, 0)


def sum_copied(grads):
    part = sum_half(grads, "dp", 0, 1)
    part = sum_half(part, "section", 0, 0)[0]
    part = sum_half(part, "mp", 0, 0)
    part = sum_far(part, 0)
    part = both_halves(part, "mp", 0, 0)
    return both_halves(part, "dp", 0, 0)


def local(
    atoms_in,
    atom_token,
    window_start,
    noise_level,
    level_table,
    single_trunk,
    pair,
    atom_gain,
    atom_qkv,
    atom_out,
    atom_agg,
    cond_weight,
    cond_bias,
    pair_weight,
    attn_in,
    attn_out,
    mlp_up,
    mlp_down,
    cotangent,
):
    section, mp = lax.axis_index("section"), lax.axis_index("mp")
    batch, half_atoms, atom_width = atoms_in.shape
    batch //= MICRO
    samples = batch // 2
    atoms = 2 * half_atoms
    tokens, width = cotangent.shape[1], cotangent.shape[2]
    single = single_trunk.shape[1]
    own_first = section * batch + mp * samples
    other_first = section * batch + (1 - mp) * samples

    own_atoms = lax.dynamic_slice_in_dim(atoms_in, own_first, samples, 0)
    other_atoms = swap(lax.dynamic_slice_in_dim(atoms_in, other_first, samples, 0), "mp")
    all_atoms = jnp.concatenate(
        [jnp.where(mp == 0, own_atoms, other_atoms), jnp.where(mp == 0, other_atoms, own_atoms)], 1
    )
    other_start = swap(window_start, "mp")
    starts = jnp.concatenate(
        [jnp.where(mp == 0, window_start, other_start), jnp.where(mp == 0, other_start, window_start)]
    )
    in_a = attn_in.reshape(width, -1)
    up_a = mlp_up.reshape(width, -1)
    in_b, out_b = fetch(in_a), fetch(attn_out)
    up_b, down_b = fetch(up_a), fetch(mlp_down)
    pair_w = jnp.concatenate([pair_weight, swap(pair_weight, "mp")], 1).T
    levels = lax.dynamic_slice_in_dim(noise_level, own_first, samples, 0)
    grad_out = lax.dynamic_slice_in_dim(cotangent, own_first, samples, 0).reshape(-1, width)

    token_ids = jnp.arange(tokens, dtype=jnp.int32)
    counts = jnp.sum((atom_token[:, None] == token_ids[None, :]).astype(WIDE), 0)
    inverse_counts = (1.0 / counts)[:, None]
    level_pick = (levels[:, None] == jnp.arange(level_table.shape[0], dtype=jnp.int32)[None, :])
    level_rows = jnp.sum(
        jnp.where(level_pick[:, :, None], level_table.astype(WIDE)[None], 0.0), 1, keepdims=True
    )
    windows = starts.shape[0]
    groups = windows // SPAN
    base = jnp.clip(
        jnp.arange(groups, dtype=jnp.int32) * (SPAN * QBLOCK) - KWIN // 2,
        0,
        atoms - KWIN - SPAN * QBLOCK,
    )
    rel = starts.reshape(groups, SPAN) - base[:, None]
    rel = jnp.broadcast_to(rel[:, None, None, :, None], (groups, 1, ATOM_HEADS, SPAN, QBLOCK))
    rel = rel.reshape(groups, 1, ATOM_HEADS * SPAN * QBLOCK)
    gain = atom_gain[None, :]
    qkv_w = atom_qkv.reshape(atom_width, -1)

    low_pair, bias = pair_bias(pair, pair_w)
    cond_w = jnp.transpose(cond_weight, (0, 2, 1, 3)).reshape(6, single, width)
    low, cond = conditioning(single_trunk, level_rows, cond_w, cond_bias.reshape(6, 1, width))
    qkv, probs, mixed, token_in = atom_front(
        all_atoms, gain, qkv_w, atom_out, atom_agg, rel, atom_token[None, :], inverse_counts
    )
    token_in = token_in.reshape(-1, width)
    inner, token_qkv, sig, heads_out, gated, token_probs, attn, middle = token_attention(
        token_in, cond, bias, in_a, in_b, attn_out, out_b
    )
    result, middle_grad, mlp_grads, cond_grad_1, cond_bias_1 = transition(
        middle, cond, grad_out, low, up_a, up_b, mlp_down, down_b
    )
    mlp_sum = sum_split(mlp_grads)
    other_result = swap(result, "mp")
    token_grad, attn_grads, cond_grad_0, cond_bias_0, bias_grad = attention_back(
        middle_grad, token_in, cond, attn, low, inner, token_qkv, sig, heads_out, gated,
        token_probs, in_a, in_b, attn_out, out_b,
    )
    attn_sum = sum_split(attn_grads)
    cond_sum = sum_copied(
        jnp.stack([cond_grad_0.reshape(-1, width), cond_grad_1.reshape(-1, width)])
    )
    atoms_grad, gain_grad, qkv_grad, out_grad, agg_grad = atom_back(
        all_atoms, gain, qkv_w, atom_out, atom_agg, atom_token[:, None], inverse_counts,
        qkv, probs, mixed, token_grad.reshape(samples, tokens, width),
    )
    pair_grad = pair_back(low_pair, bias_grad)

    lanes = atom_width
    half_width = atom_width // 2
    heads = pair_grad.shape[0]
    own_heads = heads // 2
    pair_ordered = jnp.where(
        mp == 0, pair_grad, jnp.concatenate([pair_grad[own_heads:], pair_grad[:own_heads]], 0)
    )
    pieces = [
        jnp.pad(gain_grad.reshape(2, half_width), ((0, 0), (0, lanes - half_width))).reshape(2, 1, lanes),
        qkv_grad.reshape(2, -1, lanes),
        out_grad.reshape(2, -1, lanes),
        agg_grad.reshape(2, -1, lanes),
        jnp.stack([cond_bias_0.reshape(-1, lanes), cond_bias_1.reshape(-1, lanes)]),
        pair_ordered.T.reshape(2, -1, lanes),
    ]
    sizes = [piece.shape[1] for piece in pieces]
    rows = sum(sizes)
    whole_rows = -(-rows // 512) * 512
    small = jnp.concatenate(pieces + [jnp.zeros((2, whole_rows - rows, lanes), WIDE)], 1)
    small = sum_copied(small)
    cuts = [sum(sizes[:i]) for i in range(len(sizes) + 1)]
    small = [small[cuts[i] : cuts[i + 1]] for i in range(len(sizes))]
    pair_out = small[5].reshape(half_width, heads)
    pair_out = lax.dynamic_slice_in_dim(pair_out, mp * own_heads, own_heads, 1)

    result = result.reshape(samples, tokens, width)
    other_result = other_result.reshape(samples, tokens, width)
    token_out = jnp.concatenate(
        [jnp.where(mp == 0, result, other_result), jnp.where(mp == 0, other_result, result)]
    )
    keep = lax.dynamic_slice_in_dim(atoms_grad, mp * half_atoms, half_atoms, 1)
    send = lax.dynamic_slice_in_dim(atoms_grad, (1 - mp) * half_atoms, half_atoms, 1)
    got = swap(send.astype(LOW), "mp").astype(WIDE)
    atoms_out = jnp.concatenate([jnp.where(mp == 0, keep, got), jnp.where(mp == 0, got, keep)])
    half = width // 2
    attn_local, mlp_local = attn_in.shape[2], mlp_up.shape[2]
    in_sum = jnp.transpose(attn_sum[: 4 * half].reshape(4, half, attn_local), (1, 0, 2))
    up_sum = jnp.transpose(
        mlp_sum[: 4 * half].reshape(2, mlp_local // half, half, half), (2, 0, 1, 3)
    ).reshape(half, 2, mlp_local)
    return (
        token_out.reshape(1, 1, batch, tokens, width),
        atoms_out.reshape(1, 1, batch, half_atoms, atom_width),
        small[0].reshape(lanes)[:half_width],
        small[1].reshape(half_width, 3, atom_width),
        small[2].reshape(half_width, atom_width),
        small[3].reshape(half_width, width),
        jnp.transpose(cond_sum.reshape(1, 3, single, width), (0, 2, 1, 3)).astype(WIDE),
        small[4].reshape(1, 3, width),
        pair_out,
        in_sum.astype(WIDE),
        attn_sum[4 * half :].astype(WIDE),
        up_sum.astype(WIDE),
        mlp_sum[4 * half :].astype(WIDE),
    )


def solution(mesh):
    in_specs = (
        P("dp", "mp", None),
        P(),
        P("mp"),
        P("dp"),
        P(),
        P(),
        P(),
        P(),
        P(),
        P(),
        P(),
        P(),
        P(),
        P(None, "mp"),
        P(None, None, "mp"),
        P("mp", None),
        P(None, None, "mp"),
        P("mp", None),
        P("dp", None, None),
    )
    out_specs = (
        P("dp", "section", None, None, None),
        P("dp", "section", None, "mp", None),
        P("section"),
        P("section", None, None),
        P("section", None),
        P("section", None),
        P("section", None, None, None),
        P("section", None, None),
        P("section", "mp"),
        P("section", None, "mp"),
        P("mp", "section"),
        P("section", None, "mp"),
        P("mp", "section"),
    )
    return jax.shard_map(local, mesh=mesh, in_specs=in_specs, out_specs=out_specs, check_vma=False)
```

time: 1620 us -> 487 us (0.30); the launches traced: 1590 us -> 481 us
  other arithmetic: 548 us -> 36.5 us
  matrix products: 292 us -> 0 us
  local copies, waits for them, and re-layouts: 288 us -> 66.7 us
  Pallas kernels: 0 us -> 157 us
  waiting for transfers between devices: 313 us -> 165 us
  blocking collectives: 97.9 us -> 0 us
  starting transfers between devices: 34 us -> 54.3 us
    scatter-add x6 -> x0, other arithmetic: 383 us -> none  [the longest x2 377 us: local(): grad_ext = jnp.zeros((batch, local_atoms + KWIN, 2, CA), wide_type).at[:,...]
    dot_general x75 -> x0, matrix products: 276 us -> none  [the longest x2 17.9 us: local(): jnp.einsum('at,btd->bad', member, atom_grad_tokens, precision=HIGH)]
    psum x8 -> x0, waiting for transfers between devices: 271 us -> none  [the longest x2 85.3 us: atom_tokens(): lax.psum(partial_sums.astype(jnp.bfloat16), 'mp').astype(jnp.float32)]
    pallas_call x0 -> x8, Pallas kernels: none -> 157 us  [the longest x1 35.1 us: atom_back(): pl.pallas_call(atom_back_kernel, grid=(samples,), in_specs=[sample(atoms)...]
    ppermute x13 -> x47, waiting for transfers between devices: 41.5 us -> 165 us  [swap(): return lax.ppermute(array, axis, [(i, i ^ 1 << bit) for i in range(size)])]
    psum x2 -> x0, blocking collectives: 88.3 us -> none  [the longest x1 70.5 us: local(): atom_sums = lax.psum((state[3], state[4], state[5], state[6]), ('mp', 'dp'))]
    reduce_sum x25 -> x2, other arithmetic: 63.8 us -> 0.26 us  [the longest x1 0.17 us: local(): jnp.sum((atom_token[:, None] == token_ids[None, :]).astype(WIDE), 0)]
    gather x4 -> x0, local copies, waits for them, and re-layouts: 55.2 us -> none  [atom_front(): window_kv = extended[:, rows]]
  transfers between devices with their start and end apart: 30 -> 47, of which waited for: 10 -> 27; matrix products, arithmetic and copies ran while one was open for 57% -> 13% of each run, Pallas kernels for 0% -> 9%
where the time goes in v1:
time: 487 us; the launch traced here: 481 us
  waiting for transfers between devices  165 us (34%)
  Pallas kernels  157 us (32%)
  local copies, waits for them, and re-layouts  66.7 us (14%)
  starting transfers between devices  54.3 us (11%)
  other arithmetic  36.5 us (7%)
    ppermute x47, waiting for transfers between devices, swap(): return lax.ppermute(array, axis, [(i, i ^ 1 << bit) for i in range(size)])  165 us
    ppermute x47, starting transfers between devices, swap(): return lax.ppermute(array, axis, [(i, i ^ 1 << bit) for i in range(size)])  54.3 us
    pallas_call x1, Pallas kernels, atom_back(): pl.pallas_call(atom_back_kernel, grid=(samples,), in_specs=[sample(atoms)...  35.1 us
    unnamed x122, local copies, waits for them, and re-layouts  29.9 us
    pallas_call x1, Pallas kernels, atom_front(): pl.pallas_call(atom_front_kernel, grid=(samples,), in_specs=[sample(count...  28 us
    pallas_call x1, Pallas kernels, attention_back(): pl.pallas_call(attention_back_kernel, grid=(1,), in_specs=[whole(middle_g...  27.8 us
    pallas_call x1, Pallas kernels, token_attention(): pl.pallas_call(token_attention_kernel, grid=(1,), in_specs=[whole(tokens....  20 us
    pallas_call x1, Pallas kernels, transition(): pl.pallas_call(transition_kernel, grid=(1,), in_specs=[whole(middle.shape...  19.1 us
  transfers between devices with their start and end apart: 47, of which 27 were waited for; matrix products, arithmetic and copies ran while one was open for 13% of the time, Pallas kernels for 9%

profile of v1, /device:TPU:0, one launch (start us, length us, event | category | flops | bytes accessed | tf_op | source)
XLA Modules:
  0.0 480.9 jit_solution(7131221777788002021)
XLA Ops:
  2.5 3.0 collective-permute-start
  5.5 3.5 copy.85
  25.1 3.3 conditioning.1
  33.0 14.0 %collective-permute-done.2 = bf16[128,8]{0,1:T(8,128)(2,1)S(1)} collective-permute-done((bf16[128,8]{0,1:T(8,128)(2,1)S(1)}, bf16[128,8]{0,1:T(8,128)(2,1)S(1)}, u32[]{:S(2)}, u32[]{:S(2)}) %collective-permute-start.2) | collective-permute-done | bytes 2080 | tf_op jit(solution)/shard_map/ppermute | solution.py:671
  49.0 2.9 copy-done.8
  51.9 12.4 %pair_bias.1 = (bf16[160,160,128]{2,1,0:T(8,128)(2,1)S(1)}, f32[16,160,160]{2,1,0:T(8,128)S(1)}) custom-call(bf16[160,160,128]{2,1,0:T(8,128)(2,1)S(1)} %copy-done.8, bf16[16,128]{1,0:T(8,128)(2,1)S(1)} %maximum_bitcast_fusion.2.weight_ref), custom_call_target="tpu_custom_call" | custom-call | flops 20000000000 | bytes 16000000 | tf_op jit(solution)/shard_map/pair_bias/pallas_call | solution.py:74
  64.3 2.8 copy-done.20
  69.2 14.2 %collective-permute-done.9 = bf16[384,768]{1,0:T(8,128)(2,1)S(1)} collective-permute-done((bf16[384,768]{1,0:T(8,128)(2,1)S(1)}, bf16[384,768]{1,0:T(8,128)(2,1)S(1)}, u32[]{:S(2)}, u32[]{:S(2)}) %collective-permute-start.9) | collective-permute-done | bytes 589856 | tf_op jit(solution)/shard_map/ppermute | solution.py:671
  83.9 28.0 %atom_front.1 = (bf16[2,1280,384]{2,1,0:T(8,128)(2,1)S(1)}, bf16[2,20,192,256]{3,2,1,0:T(8,128)(2,1)}, bf16[2,1280,128]{2,1,0:T(8,128)(2,1)S(1)}, bf16[2,160,768]{2,1,0:T(8,128)(2,1)S(1)}) custom-call(bf16[2,1280,128]{2,1,0:T(8,128)(2,1)S(1)} %pad_maximum_fusion.9.atoms_ref, bf16[1,128]{1,0:T(2,128)(2,1)S(1)} %bitcast.79, ...), custom_call_target="tpu_custom_call" | custom-call | flops 20000000000 | bytes 12000000 | tf_op jit(solution)/shard_map/atom_front/pallas_call | solution.py:251
  121.7 20.0 %token_attention.1 = (bf16[320,768]{1,0:T(8,128)(2,1)}, bf16[2,320,1152]{2,1,0:T(8,128)(2,1)}, f32[2,320,384]{2,1,0:T(8,128)}, f32[2,320,384]{2,1,0:T(8,128)}, b...) custom-call(bf16[320,768]{1,0:T(8,128)(2,1)} %bitcast.81, ...), custom_call_target="tpu_custom_call" | custom-call | flops 40000000000 | bytes 20000000 | tf_op jit(solution)/shard_map/token_attention/pallas_call | solution.py:450
  141.7 19.1 %transition.1 = (bf16[320,768]{1,0:T(8,128)(2,1)}, f32[320,768]{1,0:T(8,128)}, bf16[2,2,2304,384]{3,2,1,0:T(8,128)(2,1)}, bf16[3,384,768]{2,1,0:T(8,128)(2,1)}, f32[3,1,768]{2,1,0:T(1,128)}) custom-call(f32[320,768]{1,0:T(8,128)} %get-tuple-element.47.middle_ref, f32[6,320,768]{2,1,0:T(8,128)} %copy-done.19, f32[6,320,768]{2,1,0:T(8,128)} %copy-done.19, ...), custom_call_target="tpu_custom_call" | custom-call | flops 60000002048 | bytes 20000000 | tf_op jit(solution)/shard_map/transition/pallas_call | solution.py:542
  160.8 27.8 %attention_back.1 = (bf16[320,768]{1,0:T(8,128)(2,1)}, bf16[2,2,1920,384]{3,2,1,0:T(8,128)(2,1)}, bf16[3,384,768]{2,1,0:T(8,128)(2,1)}, f32[3,1,768]{2,1,0:T(1,128)}, f32[16,160,160]{2,1,0:T(8,128)}) custom-call(f32[320,768]{1,0:T(8,128)} %get-tuple-element.53.middle_grad_ref, bf16[320,768]{1,0:T(8,128)(2,1)} %bitcast.82, f32[6,320,768]{2,1,0:T(8,128)} %copy-done.19, ...), custom_call_target="tpu_custom_call" | custom-call | flops 60000002048 | bytes 24000000 | tf_op jit(solution)/shard_map/attention_back/pallas_call | solution.py:654
  188.6 2.9 copy-done.21
  193.2 10.8 %pair_back.1 = f32[16,128]{1,0:T(8,128)S(1)} custom-call(bf16[160,160,128]{2,1,0:T(8,128)(2,1)S(1)} %copy-done.21, f32[16,160,160]{2,1,0:T(8,128)S(1)} %copy-done.22), custom_call_target="tpu_custom_call" | custom-call | flops 10000000000 | bytes 9000000 | tf_op jit(solution)/shard_map/pair_back/pallas_call | solution.py:111
  207.5 35.1 %atom_back.1 = (f32[2,1280,128]{2,1,0:T(8,128)S(1)}, f32[1,128]{1,0:T(1,128)S(1)}, f32[128,384]{1,0:T(8,128)S(1)}, f32[128,128]{1,0:T(8,128)S(1)}, f32[128,768]{1,0:T(8,128)S(1)}) custom-call(bf16[2,1280,128]{2,1,0:T(8,128)(2,1)S(1)} %copy-done.3, bf16[1,128]{1,0:T(2,128)(2,1)S(1)} %bitcast.80, bf16[128,384]{1,0:T(8,128)(2,1)S(1)} %copy-done.5, ...), custom_call_target="tpu_custom_call" | custom-call | flops 40000000000 | bytes 12000000 | tf_op jit(solution)/shard_map/atom_back/pallas_call | solution.py:355
  260.2 3.1 collective-permute-done.15
  269.4 6.5 %collective-permute-done.12 = bf16[2,640,128]{2,1,0:T(8,128)(2,1)S(1)} collective-permute-done((bf16[2,640,128]{2,1,0:T(8,128)(2,1)S(1)}, bf16[2,640,128]{2,1,0:T(8,128)(2,1)S(1)}, u32[]{:S(2)}, u32[]{:S(2)}) %collective-permute-start.12) | collective-permute-done | bytes 327712 | tf_op jit(solution)/shard_map/ppermute | solution.py:671
  292.9 3.2 collective-permute-done.20
  296.1 3.9 collective-permute-done.23
  302.9 5.8 %collective-permute-done.24 = bf16[288,768]{1,0:T(8,128)(2,1)S(1)} collective-permute-done((bf16[288,768]{1,0:T(8,128)(2,1)S(1)}, bf16[288,768]{1,0:T(8,128)(2,1)S(1)}, u32[]{:S(2)}, u32[]{:S(2)}) %collective-permute-start.24) | collective-permute-done | bytes 442400 | tf_op jit(solution)/shard_map/ppermute | solution.py:671
  335.9 3.2 collective-permute-done.28
  341.6 7.1 %collective-permute-done.32 = bf16[2,960,384]{2,1,0:T(8,128)(2,1)} collective-permute-done((bf16[2,960,384]{2,1,0:T(8,128)(2,1)}, bf16[2,960,384]{2,1,0:T(8,128)(2,1)}, u32[]{:S(2)}, u32[]{:S(2)}) %collective-permute-start.32) | collective-permute-done | bytes 1474592 | tf_op jit(solution)/shard_map/ppermute | solution.py:671
  353.4 30.1 %collective-permute-done.40 = bf16[2,1152,384]{2,1,0:T(8,128)(2,1)} collective-permute-done((bf16[2,1152,384]{2,1,0:T(8,128)(2,1)}, bf16[2,1152,384]{2,1,0:T(8,128)(2,1)}, u32[]{:S(2)}, u32[]{:S(2)}) %collective-permute-start.40) | collective-permute-done | bytes 1769504 | tf_op jit(solution)/shard_map/ppermute | solution.py:671
  394.0 5.8 %collective-permute-done.41 = bf16[1,1152,384]{2,1,0:T(8,128)(2,1)S(1)} collective-permute-done((bf16[1,1152,384]{2,1,0:T(8,128)(2,1)S(1)}, bf16[1,1152,384]{2,1,0:T(8,128)(2,1)S(1)}, u32[]{:S(2)}, u32[]{:S(2)}) %collective-permute-start.41) | collective-permute-done | bytes 884768 | tf_op jit(solution)/shard_map/ppermute | solution.py:671
  406.6 10.3 %collective-permute-done.42 = bf16[576,384]{1,0:T(8,128)(2,1)S(1)} collective-permute-done((bf16[576,384]{1,0:T(8,128)(2,1)S(1)}, bf16[576,384]{1,0:T(8,128)(2,1)S(1)}, u32[]{:S(2)}, u32[]{:S(2)}) %collective-permute-start.42) | collective-permute-done | bytes 442400 | tf_op jit(solution)/shard_map/ppermute | solution.py:671
  420.3 14.0 %collective-permute-done.43 = bf16[288,384]{1,0:T(8,128)(2,1)S(1)} collective-permute-done((bf16[288,384]{1,0:T(8,128)(2,1)S(1)}, bf16[288,384]{1,0:T(8,128)(2,1)S(1)}, u32[]{:S(2)}, u32[]{:S(2)}) %collective-permute-start.43) | collective-permute-done | bytes 221216 | tf_op jit(solution)/shard_map/ppermute | solution.py:671
  434.4 8.5 %collective-permute-done.36 = bf16[240,384]{1,0:T(8,128)(2,1)S(1)} collective-permute-done((bf16[240,384]{1,0:T(8,128)(2,1)S(1)}, bf16[240,384]{1,0:T(8,128)(2,1)S(1)}, u32[]{:S(2)}, u32[]{:S(2)}) %collective-permute-start.36) | collective-permute-done | bytes 184352 | tf_op jit(solution)/shard_map/ppermute | solution.py:671
  443.1 4.1 collective-permute-done.44
  447.5 7.6 %collective-permute-done.37 = bf16[480,384]{1,0:T(8,128)(2,1)S(1)} collective-permute-done((bf16[480,384]{1,0:T(8,128)(2,1)S(1)}, bf16[480,384]{1,0:T(8,128)(2,1)S(1)}, u32[]{:S(2)}, u32[]{:S(2)}) %collective-permute-start.37) | collective-permute-done | bytes 368672 | tf_op jit(solution)/shard_map/ppermute | solution.py:671
  455.4 9.1 %collective-permute-done.45 = bf16[576,384]{1,0:T(8,128)(2,1)S(1)} collective-permute-done((bf16[576,384]{1,0:T(8,128)(2,1)S(1)}, bf16[576,384]{1,0:T(8,128)(2,1)S(1)}, u32[]{:S(2)}, u32[]{:S(2)}) %collective-permute-start.45) | collective-permute-done | bytes 442400 | tf_op jit(solution)/shard_map/ppermute | solution.py:671
  472.5 3.2 copy.82
  475.7 4.7 reshape.227
  (339 shorter events, 148.6 us)
Async XLA Ops:
  2.5 64.7 %collective-permute-start = (bf16[2,640,128]{2,1,0:T(8,128)(2,1)}, bf16[2,640,128]{2,1,0:T(8,128)(2,1)}, u32[]{:S(2)}, u32[]{:S(2)}) collective-permute-start(bf16[2,640,128]{2,1,0:T(8,128)(2,1)} %constant_dynamic-slice_fusion.19), channel_id=1, source_target_pairs={{0,8},{8,0},{1,9},{9,1},{2,10},{10,2},{3,11},{11,3},{4,12},{12,4},... | collective-permute-start | bytes 983048 | tf_op jit(solution)/shard_map/ppermute | solution.py:671
  5.5 26.0 %collective-permute-start.1 = (s32[20]{0:T(128)}, s32[20]{0:T(128)}, u32[]{:S(2)}, u32[]{:S(2)}) collective-permute-start(s32[20]{0:T(128)} %param.21), channel_id=1, source_target_pairs={{0,8},{8,0},{1,9},{9,1},{2,10},{10,2},{3,11},{11,3},{4,12},{12,4},... | collective-permute-start | bytes 248 | tf_op jit(solution)/shard_map/ppermute | solution.py:671
  11.5 71.9 %collective-permute-start.3 = (bf16[384,1536]{1,0:T(8,128)(2,1)}, bf16[384,1536]{1,0:T(8,128)(2,1)}, u32[]{:S(2)}, u32[]{:S(2)}) collective-permute-start(bf16[384,1536]{1,0:T(8,128)(2,1)} %constant_dynamic-slice_fusion.18), channel_id=1, source_target_pairs={{0,8},{8,0},{1,9},{9,1},{2,10},{10,2},{3,11},{11,3},{4,12},{12,4},... | collective-permute-start | bytes 3538952 | tf_op jit(solution)/shard_map/ppermute | solution.py:671
  14.2 52.9 %collective-permute-start.5 = (bf16[192,768]{1,0:T(8,128)(2,1)}, bf16[192,768]{1,0:T(8,128)(2,1)}, u32[]{:S(2)}, u32[]{:S(2)}) collective-permute-start(bf16[192,768]{1,0:T(8,128)(2,1)} %constant_dynamic-slice_fusion.17), channel_id=1, source_target_pairs={{0,8},{8,0},{1,9},{9,1},{2,10},{10,2},{3,11},{11,3},{4,12},{12,4},... | collective-permute-start | bytes 884744 | tf_op jit(solution)/shard_map/ppermute | solution.py:671
  14.2 32.8 %collective-permute-start.2 = (bf16[128,8]{0,1:T(8,128)(2,1)S(1)}, bf16[128,8]{0,1:T(8,128)(2,1)S(1)}, u32[]{:S(2)}, u32[]{:S(2)}) collective-permute-start(bf16[128,8]{0,1:T(8,128)(2,1)S(1)} %copy-done.52), channel_id=1, source_target_pairs={{0,8},{8,0},{1,9},{9,1},{2,10},{10,2},{3,11},{11,3},{4,12},{12,4},... | collective-permute-start | bytes 6152 | tf_op jit(solution)/shard_map/ppermute | solution.py:671
  31.6 82.6 %collective-permute-start.7 = (bf16[384,1536]{1,0:T(8,128)(2,1)}, bf16[384,1536]{1,0:T(8,128)(2,1)}, u32[]{:S(2)}, u32[]{:S(2)}) collective-permute-start(bf16[384,1536]{1,0:T(8,128)(2,1)} %constant_dynamic-slice_fusion.15), channel_id=1, source_target_pairs={{0,8},{8,0},{1,9},{9,1},{2,10},{10,2},{3,11},{11,3},{4,12},{12,4},... | collective-permute-start | bytes 3538952 | tf_op jit(solution)/shard_map/ppermute | solution.py:671
  47.0 36.4 %collective-permute-start.9 = (bf16[384,768]{1,0:T(8,128)(2,1)S(1)}, bf16[384,768]{1,0:T(8,128)(2,1)S(1)}, u32[]{:S(2)}, u32[]{:S(2)}) collective-permute-start(bf16[384,768]{1,0:T(8,128)(2,1)S(1)} %constant_dynamic-slice_fusion.14), channel_id=1, source_target_pairs={{0,8},{8,0},{1,9},{9,1},{2,10},{10,2},{3,11},{11,3},{4,12},{12,4},... | collective-permute-start | bytes 1769480 | tf_op jit(solution)/shard_map/ppermute | solution.py:671
  67.1 44.9 %collective-permute-start.6 = (bf16[192,768]{1,0:T(8,128)(2,1)}, bf16[192,768]{1,0:T(8,128)(2,1)S(1)}, u32[]{:S(2)}, u32[]{:S(2)}) collective-permute-start(bf16[192,768]{1,0:T(8,128)(2,1)} %collective-permute-done.5), channel_id=1, source_target_pairs={{0,1},{1,0},{2,3},{3,2},{4,5},{5,4},{6,7},{7,6},{8,9},{9,8},{10,11... | collective-permute-start | bytes 884744 | tf_op jit(solution)/shard_map/ppermute | solution.py:671
  83.4 30.8 %collective-permute-start.10 = (bf16[384,768]{1,0:T(8,128)(2,1)S(1)}, bf16[384,768]{1,0:T(8,128)(2,1)S(1)}, u32[]{:S(2)}, u32[]{:S(2)}) collective-permute-start(bf16[384,768]{1,0:T(8,128)(2,1)S(1)} %collective-permute-done.9), channel_id=1, source_target_pairs={{0,1},{1,0},{2,3},{3,2},{4,5},{5,4},{6,7},{7,6},{8,9},{9,8},{10,11... | collective-permute-start | bytes 1769480 | tf_op jit(solution)/shard_map/ppermute | solution.py:671
  83.4 32.0 %collective-permute-start.4 = (bf16[384,1536]{1,0:T(8,128)(2,1)}, bf16[384,1536]{1,0:T(8,128)(2,1)S(1)}, u32[]{:S(2)}, u32[]{:S(2)}) collective-permute-start(bf16[384,1536]{1,0:T(8,128)(2,1)} %collective-permute-done.3), channel_id=1, source_target_pairs={{0,1},{1,0},{2,3},{3,2},{4,5},{5,4},{6,7},{7,6},{8,9},{9,8},{10,11... | collective-permute-start | bytes 3538952 | tf_op jit(solution)/shard_map/ppermute | solution.py:671
  253.8 64.4 %collective-permute-start.39 = (bf16[2,2,1152,384]{3,2,1,0:T(8,128)(2,1)S(1)}, bf16[2,2,1152,384]{3,2,1,0:T(8,128)(2,1)S(1)}, u32[]{:S(2)}, u32[]{:S(2)}) collective-permute-start(bf16[2,2,1152,384]{3,2,1,0:T(8,128)(2,1)S(1)} %constant_dynamic-slice_fusion.2), channel_id=1, source_target_pairs={{0,1},{1,0},{2,3},{3,2},{4,5},{5,4},{6,7},{7,6},{8,9},{9,8},{10,11... | collective-permute-start | bytes 10616840 | tf_op jit(solution)/shard_map/ppermute | solution.py:671
  255.3 46.8 %collective-permute-start.31 = (bf16[2,2,960,384]{3,2,1,0:T(8,128)(2,1)S(1)}, bf16[2,2,960,384]{3,2,1,0:T(8,128)(2,1)S(1)}, u32[]{:S(2)}, u32[]{:S(2)}) collective-permute-start(bf16[2,2,960,384]{3,2,1,0:T(8,128)(2,1)S(1)} %constant_dynamic-slice_fusion.5), channel_id=1, source_target_pairs={{0,1},{1,0},{2,3},{3,2},{4,5},{5,4},{6,7},{7,6},{8,9},{9,8},{10,11... | collective-permute-start | bytes 8847368 | tf_op jit(solution)/shard_map/ppermute | solution.py:671
  260.1 25.8 %collective-permute-start.22 = (bf16[2,576,768]{2,1,0:T(8,128)(2,1)S(1)}, bf16[2,576,768]{2,1,0:T(8,128)(2,1)S(1)}, u32[]{:S(2)}, u32[]{:S(2)}) collective-permute-start(bf16[2,576,768]{2,1,0:T(8,128)(2,1)S(1)} %fusion.2), channel_id=1, source_target_pairs={{0,1},{1,0},{2,3},{3,2},{4,5},{5,4},{6,7},{7,6},{8,9},{9,8},{10,11... | collective-permute-start | bytes 5308424 | tf_op jit(solution)/shard_map/ppermute | solution.py:671
  265.2 10.7 %collective-permute-start.12 = (bf16[2,640,128]{2,1,0:T(8,128)(2,1)S(1)}, bf16[2,640,128]{2,1,0:T(8,128)(2,1)S(1)}, u32[]{:S(2)}, u32[]{:S(2)}) collective-permute-start(bf16[2,640,128]{2,1,0:T(8,128)(2,1)S(1)} %dynamic-slice_convert_fusion), channel_id=1, source_target_pairs={{0,8},{8,0},{1,9},{9,1},{2,10},{10,2},{3,11},{11,3},{4,12},{12,4},... | collective-permute-start | bytes 983048 | tf_op jit(solution)/shard_map/ppermute | solution.py:671
  267.6 20.6 %collective-permute-start.11 = (bf16[320,768]{1,0:T(8,128)(2,1)S(1)}, bf16[320,768]{1,0:T(8,128)(2,1)S(1)}, u32[]{:S(2)}, u32[]{:S(2)}) collective-permute-start(bf16[320,768]{1,0:T(8,128)(2,1)S(1)} %copy-done.42), channel_id=1, source_target_pairs={{0,8},{8,0},{1,9},{9,1},{2,10},{10,2},{3,11},{11,3},{4,12},{12,4},... | collective-permute-start | bytes 1474568 | tf_op jit(solution)/shard_map/ppermute | solution.py:671
  286.4 13.6 %collective-permute-start.23 = (bf16[1,576,768]{2,1,0:T(8,128)(2,1)S(1)}, bf16[1,576,768]{2,1,0:T(8,128)(2,1)S(1)}, u32[]{:S(2)}, u32[]{:S(2)}) collective-permute-start(bf16[1,576,768]{2,1,0:T(8,128)(2,1)S(1)} %constant_dynamic-slice_fusion.9), channel_id=1, source_target_pairs={{0,16},{16,0},{1,17},{17,1},{2,18},{18,2},{3,19},{19,3},{4,20},{20... | collective-permute-start | bytes 2654216 | tf_op jit(solution)/shard_map/ppermute | solution.py:671
  302.0 20.4 %collective-permute-start.21 = (f32[512,128]{1,0:T(8,128)S(1)}, f32[512,128]{1,0:T(8,128)S(1)}, u32[]{:S(2)}, u32[]{:S(2)}) collective-permute-start(f32[512,128]{1,0:T(8,128)S(1)} %pad_maximum_fusion.14), channel_id=1, source_target_pairs={{0,1},{1,0},{2,3},{3,2},{4,5},{5,4},{6,7},{7,6},{8,9},{9,8},{10,11... | collective-permute-start | bytes 786440 | tf_op jit(solution)/shard_map/ppermute | solution.py:671
  312.7 36.0 %collective-permute-start.32 = (bf16[2,960,384]{2,1,0:T(8,128)(2,1)}, bf16[2,960,384]{2,1,0:T(8,128)(2,1)}, u32[]{:S(2)}, u32[]{:S(2)}) collective-permute-start(bf16[2,960,384]{2,1,0:T(8,128)(2,1)} %slice_bitcast_fusion.2), channel_id=1, source_target_pairs={{0,8},{8,0},{1,9},{9,1},{2,10},{10,2},{3,11},{11,3},{4,12},{12,4},... | collective-permute-start | bytes 4423688 | tf_op jit(solution)/shard_map/ppermute | solution.py:671
  320.6 62.9 %collective-permute-start.40 = (bf16[2,1152,384]{2,1,0:T(8,128)(2,1)}, bf16[2,1152,384]{2,1,0:T(8,128)(2,1)}, u32[]{:S(2)}, u32[]{:S(2)}) collective-permute-start(bf16[2,1152,384]{2,1,0:T(8,128)(2,1)} %slice_bitcast_fusion), channel_id=1, source_target_pairs={{0,8},{8,0},{1,9},{9,1},{2,10},{10,2},{3,11},{11,3},{4,12},{12,4},... | collective-permute-start | bytes 5308424 | tf_op jit(solution)/shard_map/ppermute | solution.py:671
  340.1 49.6 %collective-permute-start.29 = (bf16[288,768]{1,0:T(8,128)(2,1)}, bf16[288,768]{1,0:T(8,128)(2,1)}, u32[]{:S(2)}, u32[]{:S(2)}) collective-permute-start(bf16[288,768]{1,0:T(8,128)(2,1)} %pad_maximum_fusion.11), channel_id=1, source_target_pairs={{0,8},{8,0},{1,9},{9,1},{2,10},{10,2},{3,11},{11,3},{4,12},{12,4},... | collective-permute-start | bytes 1327112 | tf_op jit(solution)/shard_map/ppermute | solution.py:671
  352.0 39.2 %collective-permute-start.33 = (bf16[1,960,384]{2,1,0:T(8,128)(2,1)}, bf16[1,960,384]{2,1,0:T(8,128)(2,1)}, u32[]{:S(2)}, u32[]{:S(2)}) collective-permute-start(bf16[1,960,384]{2,1,0:T(8,128)(2,1)} %constant_dynamic-slice_fusion.4), channel_id=1, source_target_pairs={{0,16},{16,0},{1,17},{17,1},{2,18},{18,2},{3,19},{19,3},{4,20},{20... | collective-permute-start | bytes 2211848 | tf_op jit(solution)/shard_map/ppermute | solution.py:671
  386.7 13.1 %collective-permute-start.41 = (bf16[1,1152,384]{2,1,0:T(8,128)(2,1)S(1)}, bf16[1,1152,384]{2,1,0:T(8,128)(2,1)S(1)}, u32[]{:S(2)}, u32[]{:S(2)}) collective-permute-start(bf16[1,1152,384]{2,1,0:T(8,128)(2,1)S(1)} %constant_dynamic-slice_fusion.1), channel_id=1, source_target_pairs={{0,16},{16,0},{1,17},{17,1},{2,18},{18,2},{3,19},{19,3},{4,20},{20... | collective-permute-start | bytes 2654216 | tf_op jit(solution)/shard_map/ppermute | solution.py:671
  391.0 10.5 %collective-permute-start.30 = (bf16[576,768]{1,0:T(8,128)(2,1)S(1)}, bf16[576,768]{1,0:T(8,128)(2,1)S(1)}, u32[]{:S(2)}, u32[]{:S(2)}) collective-permute-start(bf16[576,768]{1,0:T(8,128)(2,1)S(1)} %pad_maximum_fusion.6), channel_id=1, source_target_pairs={{0,1},{1,0},{2,3},{3,2},{4,5},{5,4},{6,7},{7,6},{8,9},{9,8},{10,11... | collective-permute-start | bytes 2654216 | tf_op jit(solution)/shard_map/ppermute | solution.py:671
  392.6 11.5 %collective-permute-start.34 = (bf16[480,384]{1,0:T(8,128)(2,1)S(1)}, bf16[480,384]{1,0:T(8,128)(2,1)S(1)}, u32[]{:S(2)}, u32[]{:S(2)}) collective-permute-start(bf16[480,384]{1,0:T(8,128)(2,1)S(1)} %dynamic-slice_bitcast_fusion.2), channel_id=1, source_target_pairs={{0,2},{1,3},{2,0},{3,1},{4,6},{5,7},{6,4},{7,5},{8,10},{9,11},{10,... | collective-permute-start | bytes 1105928 | tf_op jit(solution)/shard_map/ppermute | solution.py:671
  400.2 16.8 %collective-permute-start.42 = (bf16[576,384]{1,0:T(8,128)(2,1)S(1)}, bf16[576,384]{1,0:T(8,128)(2,1)S(1)}, u32[]{:S(2)}, u32[]{:S(2)}) collective-permute-start(bf16[576,384]{1,0:T(8,128)(2,1)S(1)} %dynamic-slice_bitcast_fusion), channel_id=1, source_target_pairs={{0,2},{1,3},{2,0},{3,1},{4,6},{5,7},{6,4},{7,5},{8,10},{9,11},{10,... | collective-permute-start | bytes 1327112 | tf_op jit(solution)/shard_map/ppermute | solution.py:671
  404.2 14.1 %collective-permute-start.35 = (bf16[240,384]{1,0:T(8,128)(2,1)S(1)}, bf16[240,384]{1,0:T(8,128)(2,1)S(1)}, u32[]{:S(2)}, u32[]{:S(2)}) collective-permute-start(bf16[240,384]{1,0:T(8,128)(2,1)S(1)} %constant_dynamic-slice_fusion.3), channel_id=1, source_target_pairs={{0,4},{1,5},{2,6},{3,7},{4,0},{5,1},{6,2},{7,3},{8,12},{9,13},{10,... | collective-permute-start | bytes 552968 | tf_op jit(solution)/shard_map/ppermute | solution.py:671
  417.1 17.1 %collective-permute-start.43 = (bf16[288,384]{1,0:T(8,128)(2,1)S(1)}, bf16[288,384]{1,0:T(8,128)(2,1)S(1)}, u32[]{:S(2)}, u32[]{:S(2)}) collective-permute-start(bf16[288,384]{1,0:T(8,128)(2,1)S(1)} %constant_dynamic-slice_fusion), channel_id=1, source_target_pairs={{0,4},{1,5},{2,6},{3,7},{4,0},{5,1},{6,2},{7,3},{8,12},{9,13},{10,... | collective-permute-start | bytes 663560 | tf_op jit(solution)/shard_map/ppermute | solution.py:671
  418.4 24.5 %collective-permute-start.36 = (bf16[240,384]{1,0:T(8,128)(2,1)S(1)}, bf16[240,384]{1,0:T(8,128)(2,1)S(1)}, u32[]{:S(2)}, u32[]{:S(2)}) collective-permute-start(bf16[240,384]{1,0:T(8,128)(2,1)S(1)} %add_convert_fusion.8), channel_id=1, source_target_pairs={{0,4},{1,5},{2,6},{3,7},{4,0},{5,1},{6,2},{7,3},{8,12},{9,13},{10,... | collective-permute-start | bytes 552968 | tf_op jit(solution)/shard_map/ppermute | solution.py:671
  434.3 12.9 %collective-permute-start.44 = (bf16[288,384]{1,0:T(8,128)(2,1)S(1)}, bf16[288,384]{1,0:T(8,128)(2,1)S(1)}, u32[]{:S(2)}, u32[]{:S(2)}) collective-permute-start(bf16[288,384]{1,0:T(8,128)(2,1)S(1)} %add_convert_fusion.6), channel_id=1, source_target_pairs={{0,4},{1,5},{2,6},{3,7},{4,0},{5,1},{6,2},{7,3},{8,12},{9,13},{10,... | collective-permute-start | bytes 663560 | tf_op jit(solution)/shard_map/ppermute | solution.py:671
  443.0 12.0 %collective-permute-start.37 = (bf16[480,384]{1,0:T(8,128)(2,1)S(1)}, bf16[480,384]{1,0:T(8,128)(2,1)S(1)}, u32[]{:S(2)}, u32[]{:S(2)}) collective-permute-start(bf16[480,384]{1,0:T(8,128)(2,1)S(1)} %pad_maximum_fusion.13), channel_id=1, source_target_pairs={{0,2},{1,3},{2,0},{3,1},{4,6},{5,7},{6,4},{7,5},{8,10},{9,11},{10,... | collective-permute-start | bytes 1105928 | tf_op jit(solution)/shard_map/ppermute | solution.py:671
  447.3 17.2 %collective-permute-start.45 = (bf16[576,384]{1,0:T(8,128)(2,1)S(1)}, bf16[576,384]{1,0:T(8,128)(2,1)S(1)}, u32[]{:S(2)}, u32[]{:S(2)}) collective-permute-start(bf16[576,384]{1,0:T(8,128)(2,1)S(1)} %pad_maximum_fusion.12), channel_id=1, source_target_pairs={{0,2},{1,3},{2,0},{3,1},{4,6},{5,7},{6,4},{7,5},{8,10},{9,11},{10,... | collective-permute-start | bytes 1327112 | tf_op jit(solution)/shard_map/ppermute | solution.py:671
  455.3 11.6 %collective-permute-start.38 = (bf16[960,384]{1,0:T(8,128)(2,1)S(1)}, bf16[960,384]{1,0:T(8,128)(2,1)S(1)}, u32[]{:S(2)}, u32[]{:S(2)}) collective-permute-start(bf16[960,384]{1,0:T(8,128)(2,1)S(1)} %pad_maximum_fusion.8), channel_id=1, source_target_pairs={{0,1},{1,0},{2,3},{3,2},{4,5},{5,4},{6,7},{7,6},{8,9},{9,8},{10,11... | collective-permute-start | bytes 2211848 | tf_op jit(solution)/shard_map/ppermute | solution.py:671
  (73 other events, 635.0 us)

commit v2 on v1

--- a/solution.py
+++ b/solution.py
@@ -89,41 +89,7 @@
     )(pair, weight)
 
 
-def pair_back_kernel(low_ref, grad_ref, out_ref):
-    @pl.when(pl.program_id(0) == 0)
-    def _():
-        out_ref[...] = jnp.zeros_like(out_ref)
-
-    total = out_ref[...]
-    heads = grad_ref.shape[0]
-    for i in range(low_ref.shape[0]):
-        grad = grad_ref[:, i, :]
-        high = grad.astype(LOW)
-        rest = (grad - high.astype(WIDE)).astype(LOW)
-        both = mul(jnp.concatenate([high, rest], 0), low_ref[i])
-        total += both[:heads] + both[heads:]
-    out_ref[...] = total
-
-
-def pair_back(low, grad):
-    tokens, width = low.shape[1], low.shape[2]
-    heads, block = grad.shape[0], 8
-    return pl.pallas_call(
-        pair_back_kernel,
-        grid=(tokens // block,),
-        in_specs=[
-            pl.BlockSpec((block, tokens, width), lambda i: (i, 0, 0)),
-            pl.BlockSpec((heads, block, tokens), lambda i: (0, i, 0)),
-        ],
-        out_specs=pl.BlockSpec((heads, width), lambda i: (0, 0)),
-        out_shape=sds((heads, width), WIDE),
-        compiler_params=params(24),
-        cost_estimate=cost(10e9, 9e6),
-        name="pair_back",
-    )(low, grad)
-
-
-def cond_kernel(trunk_ref, level_ref, weight_ref, bias_ref, low_ref, cond_ref):
+def cond_kernel(trunk_ref, level_ref, weight_ref, bias_ref, low_ref, first_ref, second_ref):
     step = pl.program_id(0)
     samples, tokens = level_ref.shape[0], trunk_ref.shape[0]
 
@@ -135,7 +101,15 @@
             low_ref[s * tokens : (s + 1) * tokens, :] = normed.astype(LOW)
 
     value = mul(low_ref[...], weight_ref[0]) + bias_ref[0]
-    cond_ref[0] = jnp.where(step % 3 == 1, value, sigmoid(value))
+    value = jnp.where(step % 3 == 1, value, sigmoid(value))
+
+    @pl.when(step < 3)
+    def _():
+        first_ref[0] = value
+
+    @pl.when(step >= 3)
+    def _():
+        second_ref[0] = value
 
 
 def conditioning(trunk, levels, weight, bias):
@@ -153,9 +127,10 @@
         ],
         out_specs=[
             pl.BlockSpec((rows, width), lambda i: (0, 0)),
-            pl.BlockSpec((1, rows, wide), lambda i: (i, 0, 0)),
+            pl.BlockSpec((1, rows, wide), lambda i: (jnp.minimum(i, 2), 0, 0)),
+            pl.BlockSpec((1, rows, wide), lambda i: (jnp.maximum(i, 3) - 3, 0, 0)),
         ],
-        out_shape=[sds((rows, width), LOW), sds((parts, rows, wide), WIDE)],
+        out_shape=[sds((rows, width), LOW)] + [sds((parts // 2, rows, wide), WIDE)] * 2,
         compiler_params=params(24),
         cost_estimate=cost(4e9, 10e6),
         name="conditioning",
@@ -270,119 +245,6 @@
         cost_estimate=cost(20e9, 12e6),
         name="atom_front",
     )(atoms, gain, qkv_w, out_w, agg_w, rel, ids, inverse_counts)
-
-
-def atom_back_kernel(
-    atoms_ref, gain_ref, qkv_w_ref, out_w_ref, agg_w_ref, ids_ref, inv_ref,
-    qkv_ref, probs_ref, mixed_ref, grad_ref,
-    atoms_grad_ref, gain_grad_ref, qkv_grad_ref, out_grad_ref, agg_grad_ref,
-    after_grad, mixed_grad, key_grad, value_grad, proj_grad,
-):
-    atoms, width = atoms_ref.shape[1], atoms_ref.shape[2]
-    groups, keys_in = probs_ref.shape[1], probs_ref.shape[2]
-    queries_in = SPAN * QBLOCK
-    scale = (width // ATOM_HEADS) ** (-0.5)
-
-    @pl.when(pl.program_id(0) == 0)
-    def _():
-        for ref in (gain_grad_ref, qkv_grad_ref, out_grad_ref, agg_grad_ref):
-            ref[...] = jnp.zeros_like(ref)
-
-    grad = (grad_ref[0].astype(WIDE) * inv_ref[...]).astype(LOW)
-    chunk = 256
-    token_ids = lax.broadcasted_iota(jnp.int32, (chunk, grad.shape[0]), 1)
-    for i in range(atoms // chunk):
-        rows = slice(i * chunk, (i + 1) * chunk)
-        mixed = mixed_ref[0, rows, :]
-        after = atoms_ref[0, rows, :].astype(WIDE) + mul(mixed, out_w_ref[...])
-        after_low = after.astype(LOW)
-        pre = mul(after_low, agg_w_ref[...])
-        sigma = sigmoid(pre)
-        member = jnp.where(token_ids == ids_ref[rows, :], 1.0, 0.0).astype(LOW)
-        unit_grad = mul(member, grad)
-        pre_grad = (unit_grad * (sigma * (1.0 + pre * (1.0 - sigma)))).astype(LOW)
-        agg_grad_ref[...] += mul_tn(after_low, pre_grad)
-        after_back = mul_nt(pre_grad, agg_w_ref[...])
-        after_grad[rows, :] = after_back
-        branch = after_back.astype(LOW)
-        out_grad_ref[...] += mul_tn(mixed, branch)
-        mixed_grad[rows, :] = mul_nt(branch, out_w_ref[...]).astype(LOW)
-    key_grad[...] = jnp.zeros_like(key_grad)
-    value_grad[...] = jnp.zeros_like(value_grad)
-
-    def attend(group, carry):
-        base = key_base(group, atoms)
-        first = pl.multiple_of(group * queries_in, queries_in)
-        queries = spread(qkv_ref[0, pl.ds(first, queries_in), :width], ATOM_HEADS)
-        grads = spread(mixed_grad[pl.ds(first, queries_in), :], ATOM_HEADS)
-        keys = qkv_ref[0, pl.ds(base, keys_in), width : 2 * width]
-        values = qkv_ref[0, pl.ds(base, keys_in), 2 * width :]
-        probs_low = probs_ref[0, group]
-        probs = probs_low.astype(WIDE)
-        probs_grad = mul_nt(values, grads)
-        mean = jnp.sum(probs * probs_grad, 0, keepdims=True)
-        scores_grad = (probs * (probs_grad - mean)).astype(LOW)
-        query_grad = gather_heads(mul_tn(scores_grad, keys), ATOM_HEADS)
-        proj_grad[pl.ds(first, queries_in), :width] = (query_grad * scale).astype(LOW)
-        key_grad[pl.ds(base, keys_in), :] += mul(scores_grad, queries)
-        value_grad[pl.ds(base, keys_in), :] += mul(probs_low, grads)
-        return carry
-
-    lax.fori_loop(0, groups, attend, 0)
-    proj_grad[:, width : 2 * width] = (key_grad[...] * scale).astype(LOW)
-    proj_grad[:, 2 * width :] = value_grad[...].astype(LOW)
-    gain = gain_ref[...].astype(WIDE)
-    normed, inverse = layer_norm(atoms_ref[0].astype(WIDE))
-    hidden = (normed * gain).astype(LOW)
-    proj = proj_grad[...]
-    qkv_grad_ref[...] += mul_tn(hidden, proj)
-    hidden_grad = mul_nt(proj, qkv_w_ref[...])
-    gain_grad_ref[...] += jnp.sum(hidden_grad * normed, 0, keepdims=True)
-    atoms_grad_ref[0] = after_grad[...] + norm_back(normed, inverse, hidden_grad * gain)
-
-
-def atom_back(atoms, gain, qkv_w, out_w, agg_w, ids, inverse_counts, qkv, probs, mixed, grad):
-    samples, count, width = atoms.shape
-    wide = agg_w.shape[1]
-
-    def whole(shape):
-        return pl.BlockSpec(shape, lambda i: (0,) * len(shape))
-
-    def sample(array):
-        return pl.BlockSpec((1,) + array.shape[1:], lambda i: (i,) + (0,) * (array.ndim - 1))
-
-    fixed = (gain, qkv_w, out_w, agg_w, ids, inverse_counts)
-    return pl.pallas_call(
-        atom_back_kernel,
-        grid=(samples,),
-        in_specs=[sample(atoms)]
-        + [whole(a.shape) for a in fixed]
-        + [sample(a) for a in (qkv, probs, mixed, grad)],
-        out_specs=[
-            sample(atoms),
-            whole((1, width)),
-            whole((width, 3 * width)),
-            whole((width, width)),
-            whole((width, wide)),
-        ],
-        out_shape=[
-            sds(atoms.shape, WIDE),
-            sds((1, width), WIDE),
-            sds((width, 3 * width), WIDE),
-            sds((width, width), WIDE),
-            sds((width, wide), WIDE),
-        ],
-        scratch_shapes=[
-            pltpu.VMEM((count, width), WIDE),
-            pltpu.VMEM((count, width), LOW),
-            pltpu.VMEM((count, width), WIDE),
-            pltpu.VMEM((count, width), WIDE),
-            pltpu.VMEM((count, 3 * width), LOW),
-        ],
-        compiler_params=params(48),
-        cost_estimate=cost(40e9, 12e6),
-        name="atom_back",
-    )(atoms, *fixed, qkv, probs, mixed, grad)
 
 
 def token_attention_kernel(
@@ -521,7 +383,11 @@
     )
     for k, piece in enumerate(pieces):
         piece = piece.astype(LOW)
-        cond_grad_ref[k] = mul(low_t, piece).astype(LOW)
+        rows = slice(k * low_t.shape[0], (k + 1) * low_t.shape[0])
+        for h in range(2):
+            cond_grad_ref[h, rows, :] = mul(
+                low_t, piece[:, h * half_cols : (h + 1) * half_cols]
+            ).astype(LOW)
         cond_bias_ref[k] = jnp.sum(piece.astype(WIDE), 0, keepdims=True)
 
 
@@ -536,14 +402,14 @@
         ((rows, width), LOW),
         ((rows, width), WIDE),
         ((2, 2, 4 * half + local, half), LOW),
-        ((3, low.shape[1], width), LOW),
+        ((2, 3 * low.shape[1], half), LOW),
         ((3, 1, width), WIDE),
     ]
     return pl.pallas_call(
         transition_kernel,
         grid=(1,),
         in_specs=[whole(middle.shape)]
-        + [part(i, (rows, width)) for i in (3, 4, 5)]
+        + [part(i, (rows, width)) for i in (0, 1, 2)]
         + [whole(a.shape) for a in (grad, low, up_a, up_b, down_a, down_b)],
         out_specs=[whole(shape) for shape, _ in outs],
         out_shape=[sds(*out) for out in outs],
@@ -557,27 +423,205 @@
     )(middle, cond, cond, cond, grad, low, up_a, up_b, down_a, down_b)
 
 
+def far_bits():
+    return range(1, lax.axis_size("dp").bit_length() - 1)
+
+
+class Links:
+    def __init__(self, send_sem, recv_sem):
+        self.section, self.mp = lax.axis_index("section"), lax.axis_index("mp")
+        self.dp = lax.axis_index("dp")
+        self.core = self.dp % 2
+        self.far = [self.dp // (1 << b) % 2 for b in far_bits()]
+        self.partners = [{"section": 1 - self.section}, {"mp": 1 - self.mp}]
+        self.partners.append({"dp": self.dp + 1 - 2 * self.core})
+        for b, side_of in zip(far_bits(), self.far):
+            self.partners.append({"dp": self.dp + (1 - 2 * side_of) * (1 << b)})
+        self.x, self.y, self.twin = self.partners[:3]
+        self.z = self.partners[3:]
+        self.send_sem, self.recv_sem, self.used = send_sem, recv_sem, 0
+
+    def barrier(self):
+        barrier = pltpu.get_barrier_semaphore()
+        for partner in self.partners:
+            pl.semaphore_signal(
+                barrier, inc=1, device_id=partner, device_id_type=pl.DeviceIdType.MESH
+            )
+        pl.semaphore_wait(barrier, len(self.partners))
+
+    def send(self, source, target, partner):
+        copy = pltpu.make_async_remote_copy(
+            src_ref=source,
+            dst_ref=target,
+            send_sem=self.send_sem.at[self.used],
+            recv_sem=self.recv_sem.at[self.used],
+            device_id=partner,
+            device_id_type=pl.DeviceIdType.MESH,
+        )
+        self.used += 1
+        copy.start()
+        return copy
+
+
+def splits_far(rows):
+    steps = []
+    for _ in far_bits():
+        halves = rows % 32 == 0
+        rows = rows // 2 if halves else rows
+        steps.append((rows, halves))
+    return steps
+
+
+def journey_copies(rows, shared):
+    steps = splits_far(rows)
+    return 4 + len(steps) + sum(halves for _, halves in steps) + (2 if shared else 0)
+
+
+def journey_scratch(chunks, rows, cols):
+    shapes = [(chunks, 2, 2, rows, cols), (chunks, 2, rows, cols), (chunks, rows, cols)]
+    shapes += [(chunks, size, cols) for size, _ in splits_far(rows)]
+    return [pltpu.VMEM(shape, LOW) for shape in shapes]
+
+
+def journey(links, grads, buffers, out, other_out, chunk, rows, x_first, shared):
+    near, middle, last = (buffer.at[chunk] for buffer in buffers[:3])
+    far = [buffer.at[chunk] for buffer in buffers[3:]]
+    total_rows = grads.shape[2]
+    start = links.core * (total_rows // 2) + chunk * rows
+    twin_start = (1 - links.core) * (total_rows // 2) + chunk * rows
+    mine, theirs = pl.ds(pl.multiple_of(start, 16), rows), pl.ds(pl.multiple_of(twin_start, 16), rows)
+    me, you = links.section, 1 - links.section
+    copy = links.send(grads.at[:, :, theirs, :], near, links.twin)
+    yield
+    copy.wait()
+    if x_first:
+        near[:, you] += grads[:, you, mine, :]
+        copy = links.send(near.at[:, you], middle, links.x)
+        near[:, me] += grads[:, me, mine, :]
+        yield
+        copy.wait()
+        middle[1] += near[1, me]
+        copy = links.send(middle.at[1], last, links.y)
+        middle[0] += near[0, me]
+        yield
+        copy.wait()
+        last[...] += middle[0]
+    else:
+        near[1] += grads[1, :, mine, :]
+        copy = links.send(near.at[1], middle, links.y)
+        near[0] += grads[0, :, mine, :]
+        yield
+        copy.wait()
+        middle[you] += near[0, you]
+        copy = links.send(middle.at[you], last, links.x)
+        middle[me] += near[0, me]
+        yield
+        copy.wait()
+        last[...] += middle[me]
+    held, place, size = last, start, rows
+    back = []
+    for (count, halves), bit, partner, slot in zip(splits_far(rows), links.far, links.z, far):
+        if halves:
+            give = pl.ds(pl.multiple_of((1 - bit) * count, 16), count)
+            keep = pl.ds(pl.multiple_of(bit * count, 16), count)
+            copy = links.send(held.at[give, :], slot, partner)
+            back.append((bit, partner))
+            place = place + bit * count
+        else:
+            keep = pl.ds(0, count)
+            copy = links.send(held, slot, partner)
+        yield
+        copy.wait()
+        slot[...] += held[keep, :]
+        held, size = slot, count
+    out[pl.ds(pl.multiple_of(place, 16), size), :] = held[...]
+    for bit, partner in reversed(back):
+        at = pl.ds(pl.multiple_of(place, 16), size)
+        copy = links.send(out.at[at, :], out.at[at, :], partner)
+        yield
+        copy.wait()
+        place, size = place - bit * size, 2 * size
+    copies = [links.send(out.at[mine, :], out.at[mine, :], links.twin)]
+    if shared:
+        across = links.send(out.at[mine, :], other_out.at[mine, :], links.y)
+        yield
+        across.wait()
+        copies.append(links.send(other_out.at[mine, :], other_out.at[mine, :], links.twin))
+    yield
+    for copy in copies:
+        copy.wait()
+
+
+class Flow:
+    def __init__(self, journeys, lag=1):
+        self.waiting, self.running, self.lag, self.count = list(journeys), [], lag, 0
+
+    def step(self):
+        if self.waiting and self.count % self.lag == 0:
+            self.running.append(self.waiting.pop(0))
+        self.count += 1
+        alive = []
+        for one in self.running:
+            if next(one, "end") is None:
+                alive.append(one)
+        self.running = alive
+
+    def finish(self):
+        while self.waiting or self.running:
+            self.step()
+
+
+CHUNK = 192
+
+
+def everywhere(count):
+    return [pl.BlockSpec(memory_space=pltpu.VMEM)] * count
+
+
+def remote_params(mib, number):
+    return pltpu.CompilerParams(
+        vmem_limit_bytes=mib * MIB, collective_id=number, has_side_effects=True
+    )
+
+
+def relative(half, mp):
+    return mp if half == 0 else 1 - mp
+
+
 def attention_back_kernel(
-    middle_grad_ref, tokens_ref, scale_ref, gate_ref, attn_ref, low_ref, inner_ref, qkv_ref,
+    middle_grad_ref, tokens_ref, cond_ref, attn_ref, low_ref, inner_ref, qkv_ref,
     sig_ref, heads_ref, gated_ref, probs_ref, in_a_ref, in_b_ref, out_a_ref, out_b_ref,
-    token_grad_ref, weight_grad_ref, cond_grad_ref, cond_bias_ref, bias_grad_ref,
-    proj_ref, heads_grad_ref,
+    mlp_ref, cond_grad_ref,
+    token_grad_ref, grads_ref, cond_bias_ref, bias_grad_ref, mlp_out_ref,
+    proj_ref, heads_grad_ref, *rest,
 ):
+    *buffers, send_sem, recv_sem = rest
+    links = Links(send_sem, recv_sem)
+    links.barrier()
+    chunks = mlp_ref.shape[2] // 2 // CHUNK
+    flow = Flow(
+        journey(links, mlp_ref, buffers, mlp_out_ref, None, i, CHUNK, i % 2 == 1, False)
+        for i in range(chunks)
+    )
+    flow.step()
     rows, width = tokens_ref.shape
     samples, heads, count = probs_ref.shape[0], probs_ref.shape[1], probs_ref.shape[2]
     local = in_a_ref.shape[1] // 4
     size = 2 * local // heads
     head_scale = size ** (-0.5)
     half_rows = width // 2
+    first_cond = 4 * half_rows + local
+    for h in range(2):
+        grads_ref[relative(h, links.mp), 1, first_cond:, :] = cond_grad_ref[h]
     middle_grad = middle_grad_ref[...]
-    gate = gate_ref[0]
+    gate = cond_ref[2]
     attn_grad = (middle_grad * gate).astype(LOW)
     inner_t = inner_ref[...].T
     inner_grad = None
     for half, (weight_ref, out_ref) in enumerate(((in_a_ref, out_a_ref), (in_b_ref, out_b_ref))):
         gated_t = gated_ref[half].T
         for sec in range(2):
-            weight_grad_ref[half, sec, 4 * half_rows :, :] = mul(
+            grads_ref[half, sec, 4 * half_rows : first_cond, :] = mul(
                 gated_t, attn_grad[:, sec * half_rows : (sec + 1) * half_rows]
             ).astype(LOW)
         gated_grad = mul_nt(attn_grad, out_ref[...])
@@ -585,6 +629,7 @@
         with_sig = gated_grad * sig
         heads_grad_ref[...] = with_sig.astype(LOW)
         proj_ref[:, 3 * local :] = (with_sig * heads_ref[half] * (1.0 - sig)).astype(LOW)
+        flow.step()
         for s in range(samples):
             at = slice(s * count, (s + 1) * count)
             grads = ([], [], [])
@@ -606,20 +651,24 @@
                 grads[0].append(mul(scores_grad, key) * head_scale)
                 grads[1].append(mul_tn(scores_grad, query) * head_scale)
                 grads[2].append(mul_tn(probs_low, grad))
+                if h % 4 == 3:
+                    flow.step()
             for k in range(3):
                 proj_ref[at, k * local : (k + 1) * local] = jnp.concatenate(grads[k], 1).astype(LOW)
         proj = proj_ref[...]
         for sec in range(2):
             for k in range(4):
-                weight_grad_ref[half, sec, k * half_rows : (k + 1) * half_rows, :] = mul(
+                grads_ref[half, sec, k * half_rows : (k + 1) * half_rows, :] = mul(
                     inner_t[sec * half_rows : (sec + 1) * half_rows],
                     proj[:, k * local : (k + 1) * local],
                 ).astype(LOW)
         add = mul_nt(proj, weight_ref[...])
         inner_grad = add if inner_grad is None else inner_grad + add
-    scale = scale_ref[0]
+        flow.step()
+    scale = cond_ref[0]
     normed, inverse = layer_norm(tokens_ref[...].astype(WIDE))
     token_grad_ref[...] = (middle_grad + norm_back(normed, inverse, inner_grad * scale)).astype(LOW)
+    flow.step()
     low_t = low_ref[...].T
     pieces = (
         inner_grad * normed * (scale * (1.0 - scale)),
@@ -628,42 +677,258 @@
     )
     for k, piece in enumerate(pieces):
         piece = piece.astype(LOW)
-        cond_grad_ref[k] = mul(low_t, piece).astype(LOW)
+        place = first_cond + k * low_t.shape[0]
+        for h in range(2):
+            grads_ref[relative(h, links.mp), 0, place : place + low_t.shape[0], :] = mul(
+                low_t, piece[:, h * half_rows : (h + 1) * half_rows]
+            ).astype(LOW)
         cond_bias_ref[k] = jnp.sum(piece.astype(WIDE), 0, keepdims=True)
+    flow.finish()
 
 
 def attention_back(
     middle_grad, tokens, cond, attn, low, inner, qkv, sig, heads_out, gated, probs,
-    in_a, in_b, out_a, out_b,
+    in_a, in_b, out_a, out_b, mlp_grads, cond_grads,
 ):
     rows, width = tokens.shape
     heads, count = probs.shape[1], probs.shape[2]
     local, half = in_a.shape[1] // 4, width // 2
-
-    def whole(shape):
-        return pl.BlockSpec(shape, lambda i: (0,) * len(shape))
-
+    chunks = mlp_grads.shape[2] // 2 // CHUNK
+    copies = chunks * journey_copies(CHUNK, False)
     outs = [
-        ((rows, width), LOW),
-        ((2, 2, 4 * half + local, half), LOW),
-        ((3, low.shape[1], width), LOW),
-        ((3, 1, width), WIDE),
-        ((heads, count, count), WIDE),
+        sds((rows, width), LOW),
+        sds((2, 2, 4 * half + local + 3 * low.shape[1], half), LOW),
+        sds((3, 1, width), WIDE),
+        sds((heads, count, count), WIDE),
+        sds(mlp_grads.shape[2:], LOW),
     ]
-    after = (attn, low, inner, qkv, sig, heads_out, gated, probs, in_a, in_b, out_a, out_b)
     return pl.pallas_call(
         attention_back_kernel,
-        grid=(1,),
-        in_specs=[whole(middle_grad.shape), whole(tokens.shape)]
-        + [part(i, (rows, width)) for i in (0, 2)]
-        + [whole(a.shape) for a in after],
-        out_specs=[whole(shape) for shape, _ in outs],
-        out_shape=[sds(*out) for out in outs],
-        scratch_shapes=[pltpu.VMEM((rows, 4 * local), LOW), pltpu.VMEM((rows, local), LOW)],
-        compiler_params=params(56),
+        in_specs=everywhere(17),
+        out_specs=everywhere(len(outs)),
+        out_shape=outs,
+        scratch_shapes=[
+            pltpu.VMEM((rows, 4 * local), LOW),
+            pltpu.VMEM((rows, local), LOW),
+            *journey_scratch(chunks, CHUNK, half),
+            pltpu.SemaphoreType.DMA((copies,)),
+            pltpu.SemaphoreType.DMA((copies,)),
+        ],
+        compiler_params=remote_params(60, 1),
         cost_estimate=cost(60e9, 24e6),
         name="attention_back",
-    )(middle_grad, tokens, cond, cond, *after)
+    )(
+        middle_grad, tokens, cond, attn, low, inner, qkv, sig, heads_out, gated, probs,
+        in_a, in_b, out_a, out_b, mlp_grads, cond_grads,
+    )
+
+
+SMALL_ROWS = 160
+
+
+def atom_back_kernel(
+    atoms_ref, gain_ref, qkv_w_ref, out_w_ref, agg_w_ref, ids_ref, inv_ref,
+    qkv_ref, probs_ref, mixed_ref, grad_ref, pair_ref, bias_grad_ref,
+    grads_ref, result_ref, cond_bias_a_ref, cond_bias_b_ref,
+    keep_ref, got_ref, other_result_ref, attn_out_ref, cond_out_ref, cond_other_ref,
+    small_out_ref, small_other_ref,
+    after_grad, mixed_grad, key_grad, value_grad, proj_grad, atoms_grad, send_buffer,
+    gain_grad, qkv_grad, out_grad, agg_grad, pair_grad, small, *rest,
+):
+    *buffers, send_sem, recv_sem = rest
+    links = Links(send_sem, recv_sem)
+    links.barrier()
+    samples, atoms, width = atoms_ref.shape
+    groups, keys_in = probs_ref.shape[1], probs_ref.shape[2]
+    queries_in = SPAN * QBLOCK
+    scale = (width // ATOM_HEADS) ** (-0.5)
+    cond_rows = cond_out_ref.shape[0]
+    attn_rows = grads_ref.shape[2] - cond_rows
+    attn_grads = grads_ref.at[:, :, :attn_rows, :]
+    cond_grads = grads_ref.at[:, :, attn_rows:, :]
+    number = len(buffers) // 3
+    first, second, third = (buffers[i * number : (i + 1) * number] for i in range(3))
+    journeys = [
+        journey(links, attn_grads, first, attn_out_ref, None, i, CHUNK, i % 2 == 1, False)
+        for i in range(attn_rows // 2 // CHUNK)
+    ]
+    journeys += [
+        journey(links, cond_grads, second, cond_out_ref, cond_other_ref, i, CHUNK, i % 2 == 0, True)
+        for i in range(cond_rows // 2 // CHUNK)
+    ]
+    flow = Flow(journeys)
+    flow.step()
+    result_copy = links.send(result_ref, other_result_ref, links.y)
+
+    heads = bias_grad_ref.shape[0]
+    total = jnp.zeros_like(pair_grad)
+    for i in range(pair_ref.shape[0]):
+        grad = bias_grad_ref[:, i, :]
+        high = grad.astype(LOW)
+        tail = (grad - high.astype(WIDE)).astype(LOW)
+        both = mul(jnp.concatenate([high, tail], 0), pair_ref[i])
+        total += both[:heads] + both[heads:]
+        if i % 40 == 39:
+            flow.step()
+    pair_grad[...] = total
+
+    for ref in (gain_grad, qkv_grad, out_grad, agg_grad):
+        ref[...] = jnp.zeros_like(ref)
+    chunk = 256
+    token_ids = lax.broadcasted_iota(jnp.int32, (chunk, grad_ref.shape[1]), 1)
+    atom_copies = []
+    for s in range(samples):
+        token_grad = (grad_ref[s].astype(WIDE) * inv_ref[...]).astype(LOW)
+        for i in range(atoms // chunk):
+            rows = slice(i * chunk, (i + 1) * chunk)
+            mixed = mixed_ref[s, rows, :]
+            after = atoms_ref[s, rows, :].astype(WIDE) + mul(mixed, out_w_ref[...])
+            after_low = after.astype(LOW)
+            pre = mul(after_low, agg_w_ref[...])
+            sigma = sigmoid(pre)
+            member = jnp.where(token_ids == ids_ref[rows, :], 1.0, 0.0).astype(LOW)
+            unit_grad = mul(member, token_grad)
+            pre_grad = (unit_grad * (sigma * (1.0 + pre * (1.0 - sigma)))).astype(LOW)
+            agg_grad[...] += mul_tn(after_low, pre_grad)
+            after_back = mul_nt(pre_grad, agg_w_ref[...])
+            after_grad[rows, :] = after_back
+            branch = after_back.astype(LOW)
+            out_grad[...] += mul_tn(mixed, branch)
+            mixed_grad[rows, :] = mul_nt(branch, out_w_ref[...]).astype(LOW)
+            if i % 2 == 1:
+                flow.step()
+        key_grad[...] = jnp.zeros_like(key_grad)
+        value_grad[...] = jnp.zeros_like(value_grad)
+
+        def attend(group, carry, s=s):
+            base = key_base(group, atoms)
+            start = pl.multiple_of(group * queries_in, queries_in)
+            queries = spread(qkv_ref[s, pl.ds(start, queries_in), :width], ATOM_HEADS)
+            grads = spread(mixed_grad[pl.ds(start, queries_in), :], ATOM_HEADS)
+            keys = qkv_ref[s, pl.ds(base, keys_in), width : 2 * width]
+            values = qkv_ref[s, pl.ds(base, keys_in), 2 * width :]
+            probs_low = probs_ref[s, group]
+            probs = probs_low.astype(WIDE)
+            probs_grad = mul_nt(values, grads)
+            mean = jnp.sum(probs * probs_grad, 0, keepdims=True)
+            scores_grad = (probs * (probs_grad - mean)).astype(LOW)
+            query_grad = gather_heads(mul_tn(scores_grad, keys), ATOM_HEADS)
+            proj_grad[pl.ds(start, queries_in), :width] = (query_grad * scale).astype(LOW)
+            key_grad[pl.ds(base, keys_in), :] += mul(scores_grad, queries)
+            value_grad[pl.ds(base, keys_in), :] += mul(probs_low, grads)
+            return carry
+
+        cuts = 4
+        for i in range(cuts):
+            lax.fori_loop(groups * i // cuts, groups * (i + 1) // cuts, attend, 0)
+            flow.step()
+        proj_grad[:, width : 2 * width] = (key_grad[...] * scale).astype(LOW)
+        proj_grad[:, 2 * width :] = value_grad[...].astype(LOW)
+        gain = gain_ref[...].astype(WIDE)
+        normed, inverse = layer_norm(atoms_ref[s].astype(WIDE))
+        hidden = (normed * gain).astype(LOW)
+        proj = proj_grad[...]
+        qkv_grad[...] += mul_tn(hidden, proj)
+        hidden_grad = mul_nt(proj, qkv_w_ref[...])
+        gain_grad[...] += jnp.sum(hidden_grad * normed, 0, keepdims=True)
+        atoms_grad[...] = after_grad[...] + norm_back(normed, inverse, hidden_grad * gain)
+        half = atoms // 2
+        theirs = pl.ds(pl.multiple_of((1 - links.mp) * half, 16), half)
+        send_buffer[s] = atoms_grad[theirs, :].astype(LOW)
+        atom_copies.append(links.send(send_buffer.at[s], got_ref.at[s], links.y))
+        keep_ref[s] = atoms_grad[pl.ds(pl.multiple_of(links.mp * half, 16), half), :]
+        flow.step()
+
+    wide = agg_grad.shape[1] // 2
+    rows, part_rows = width // 2, width // 4
+
+    def fill(values, cols):
+        if values.shape[1] == cols:
+            return values
+        empty = jnp.zeros((values.shape[0], cols - values.shape[1]), WIDE)
+        return jnp.concatenate([values, empty], 1)
+
+    for h in range(2):
+        to = relative(h, links.mp)
+        cols = slice(h * wide, (h + 1) * wide)
+        own_pair = jnp.where(links.mp == h, pair_grad[: heads // 2], pair_grad[heads // 2 :])
+        for sec, cond_bias_ref in enumerate((cond_bias_a_ref, cond_bias_b_ref)):
+            at = slice(sec * rows, (sec + 1) * rows)
+            small[to, sec, :rows, :] = agg_grad[at, cols].astype(LOW)
+            first_row = sec * rows + h * part_rows
+            part_at = slice(first_row, first_row + part_rows)
+            small[to, sec, rows : rows + part_rows, :] = fill(qkv_grad[part_at], wide).astype(LOW)
+            small[to, sec, rows + part_rows : 2 * rows, :] = fill(out_grad[part_at], wide).astype(LOW)
+            block = [fill(gain_grad[...], wide)]
+            block += [cond_bias_ref[k, :, cols] for k in range(3)]
+            block += [jnp.zeros((4, wide), WIDE), fill(own_pair, wide)]
+            block += [jnp.zeros((16, wide), WIDE)]
+            small[to, sec, 2 * rows :, :] = jnp.concatenate(block, 0).astype(LOW)
+    flow.waiting.append(
+        journey(
+            links, small, third, small_out_ref, small_other_ref, 0, SMALL_ROWS // 2, False, True
+        )
+    )
+    flow.finish()
+    result_copy.wait()
+    for copy in atom_copies:
+        copy.wait()
+
+
+def atom_back(
+    atoms, gain, qkv_w, out_w, agg_w, ids, inverse_counts, qkv, probs, mixed, grad,
+    low_pair, bias_grad, grads, result, cond_bias_a, cond_bias_b, cond_rows,
+):
+    samples, count, width = atoms.shape
+    wide = agg_w.shape[1]
+    cols = grads.shape[3]
+    attn_rows = grads.shape[2] - cond_rows
+    attn_chunks, cond_chunks = attn_rows // 2 // CHUNK, cond_rows // 2 // CHUNK
+    copies = attn_chunks * journey_copies(CHUNK, False) + cond_chunks * journey_copies(CHUNK, True)
+    copies += journey_copies(SMALL_ROWS // 2, True) + 1 + samples
+    outs = [
+        sds((samples, count // 2, width), WIDE),
+        sds((samples, count // 2, width), LOW),
+        sds(result.shape, LOW),
+        sds((attn_rows, cols), LOW),
+        sds((cond_rows, cols), LOW),
+        sds((cond_rows, cols), LOW),
+        sds((SMALL_ROWS, cols), LOW),
+        sds((SMALL_ROWS, cols), LOW),
+    ]
+    args = (
+        atoms, gain, qkv_w, out_w, agg_w, ids, inverse_counts, qkv, probs, mixed, grad,
+        low_pair, bias_grad, grads, result, cond_bias_a, cond_bias_b,
+    )
+    return pl.pallas_call(
+        atom_back_kernel,
+        in_specs=everywhere(len(args)),
+        out_specs=everywhere(len(outs)),
+        out_shape=outs,
+        scratch_shapes=[
+            pltpu.VMEM((count, width), WIDE),
+            pltpu.VMEM((count, width), LOW),
+            pltpu.VMEM((count, width), WIDE),
+            pltpu.VMEM((count, width), WIDE),
+            pltpu.VMEM((count, 3 * width), LOW),
+            pltpu.VMEM((count, width), WIDE),
+            pltpu.VMEM((samples, count // 2, width), LOW),
+            pltpu.VMEM((1, width), WIDE),
+            pltpu.VMEM((width, 3 * width), WIDE),
+            pltpu.VMEM((width, width), WIDE),
+            pltpu.VMEM((width, wide), WIDE),
+            pltpu.VMEM((bias_grad.shape[0], width), WIDE),
+            pltpu.VMEM((2, 2, SMALL_ROWS, cols), LOW),
+            *journey_scratch(attn_chunks, CHUNK, cols),
+            *journey_scratch(cond_chunks, CHUNK, cols),
+            *journey_scratch(1, SMALL_ROWS // 2, cols),
+            pltpu.SemaphoreType.DMA((copies,)),
+            pltpu.SemaphoreType.DMA((copies,)),
+        ],
+        compiler_params=remote_params(60, 2),
+        cost_estimate=cost(60e9, 24e6),
+        name="atom_back",
+    )(*args)
 
 
 def swap(array, axis, bit=0):
@@ -673,13 +938,6 @@
 
 def side(axis, bit=0):
     return (lax.axis_index(axis) >> bit) & 1
-
-
-def sum_half(array, axis, bit, dim):
-    size, me = array.shape[dim] // 2, side(axis, bit)
-    other = lax.dynamic_slice_in_dim(array, (1 - me) * size, size, dim)
-    mine = lax.dynamic_slice_in_dim(array, me * size, size, dim)
-    return (mine.astype(WIDE) + swap(other, axis, bit).astype(WIDE)).astype(array.dtype)
 
 
 def both_halves(array, axis, bit, dim):
@@ -688,38 +946,10 @@
     return jnp.concatenate([first, second], dim)
 
 
-def far_bits():
-    return range(1, lax.axis_size("dp").bit_length() - 1)
-
-
-def sum_far(array, dim):
-    for bit in far_bits():
-        array = sum_half(array, "dp", bit, dim)
-    for bit in reversed(far_bits()):
-        array = both_halves(array, "dp", bit, dim)
-    return array
-
-
 def fetch(weight):
     size = weight.shape[0] // 2
     own = lax.dynamic_slice_in_dim(weight, side("dp") * size, size, 0)
     return both_halves(swap(own, "mp"), "dp", 0, 0)
-
-
-def sum_split(grads):
-    part = sum_half(grads, "dp", 0, 2)
-    part = (part[0].astype(WIDE) + swap(part[1], "mp").astype(WIDE)).astype(LOW)
-    part = sum_half(part, "section", 0, 0)[0]
-    return both_halves(sum_far(part, 0), "dp", 0, 0)
-
-
-def sum_copied(grads):
-    part = sum_half(grads, "dp", 0, 1)
-    part = sum_half(part, "section", 0, 0)[0]
-    part = sum_half(part, "mp", 0, 0)
-    part = sum_far(part, 0)
-    part = both_halves(part, "mp", 0, 0)
-    return both_halves(part, "dp", 0, 0)
 
 
 def local(
@@ -792,66 +1022,35 @@
 
     low_pair, bias = pair_bias(pair, pair_w)
     cond_w = jnp.transpose(cond_weight, (0, 2, 1, 3)).reshape(6, single, width)
-    low, cond = conditioning(single_trunk, level_rows, cond_w, cond_bias.reshape(6, 1, width))
+    low, cond_a, cond_b = conditioning(
+        single_trunk, level_rows, cond_w, cond_bias.reshape(6, 1, width)
+    )
     qkv, probs, mixed, token_in = atom_front(
         all_atoms, gain, qkv_w, atom_out, atom_agg, rel, atom_token[None, :], inverse_counts
     )
     token_in = token_in.reshape(-1, width)
     inner, token_qkv, sig, heads_out, gated, token_probs, attn, middle = token_attention(
-        token_in, cond, bias, in_a, in_b, attn_out, out_b
-    )
-    result, middle_grad, mlp_grads, cond_grad_1, cond_bias_1 = transition(
-        middle, cond, grad_out, low, up_a, up_b, mlp_down, down_b
-    )
-    mlp_sum = sum_split(mlp_grads)
-    other_result = swap(result, "mp")
-    token_grad, attn_grads, cond_grad_0, cond_bias_0, bias_grad = attention_back(
-        middle_grad, token_in, cond, attn, low, inner, token_qkv, sig, heads_out, gated,
-        token_probs, in_a, in_b, attn_out, out_b,
-    )
-    attn_sum = sum_split(attn_grads)
-    cond_sum = sum_copied(
-        jnp.stack([cond_grad_0.reshape(-1, width), cond_grad_1.reshape(-1, width)])
-    )
-    atoms_grad, gain_grad, qkv_grad, out_grad, agg_grad = atom_back(
+        token_in, cond_a, bias, in_a, in_b, attn_out, out_b
+    )
+    result, middle_grad, mlp_grads, cond_grad, cond_bias_b = transition(
+        middle, cond_b, grad_out, low, up_a, up_b, mlp_down, down_b
+    )
+    token_grad, attn_grads, cond_bias_a, bias_grad, mlp_sum = attention_back(
+        middle_grad, token_in, cond_a, attn, low, inner, token_qkv, sig, heads_out, gated,
+        token_probs, in_a, in_b, attn_out, out_b, mlp_grads, cond_grad,
+    )
+    keep, got, other_result, attn_sum, cond_sum, cond_other, small, small_other = atom_back(
         all_atoms, gain, qkv_w, atom_out, atom_agg, atom_token[:, None], inverse_counts,
         qkv, probs, mixed, token_grad.reshape(samples, tokens, width),
-    )
-    pair_grad = pair_back(low_pair, bias_grad)
-
-    lanes = atom_width
-    half_width = atom_width // 2
-    heads = pair_grad.shape[0]
-    own_heads = heads // 2
-    pair_ordered = jnp.where(
-        mp == 0, pair_grad, jnp.concatenate([pair_grad[own_heads:], pair_grad[:own_heads]], 0)
-    )
-    pieces = [
-        jnp.pad(gain_grad.reshape(2, half_width), ((0, 0), (0, lanes - half_width))).reshape(2, 1, lanes),
-        qkv_grad.reshape(2, -1, lanes),
-        out_grad.reshape(2, -1, lanes),
-        agg_grad.reshape(2, -1, lanes),
-        jnp.stack([cond_bias_0.reshape(-1, lanes), cond_bias_1.reshape(-1, lanes)]),
-        pair_ordered.T.reshape(2, -1, lanes),
-    ]
-    sizes = [piece.shape[1] for piece in pieces]
-    rows = sum(sizes)
-    whole_rows = -(-rows // 512) * 512
-    small = jnp.concatenate(pieces + [jnp.zeros((2, whole_rows - rows, lanes), WIDE)], 1)
-    small = sum_copied(small)
-    cuts = [sum(sizes[:i]) for i in range(len(sizes) + 1)]
-    small = [small[cuts[i] : cuts[i + 1]] for i in range(len(sizes))]
-    pair_out = small[5].reshape(half_width, heads)
-    pair_out = lax.dynamic_slice_in_dim(pair_out, mp * own_heads, own_heads, 1)
+        low_pair, bias_grad, attn_grads, result, cond_bias_a, cond_bias_b, cond_grad.shape[1],
+    )
 
     result = result.reshape(samples, tokens, width)
     other_result = other_result.reshape(samples, tokens, width)
     token_out = jnp.concatenate(
         [jnp.where(mp == 0, result, other_result), jnp.where(mp == 0, other_result, result)]
     )
-    keep = lax.dynamic_slice_in_dim(atoms_grad, mp * half_atoms, half_atoms, 1)
-    send = lax.dynamic_slice_in_dim(atoms_grad, (1 - mp) * half_atoms, half_atoms, 1)
-    got = swap(send.astype(LOW), "mp").astype(WIDE)
+    got = got.astype(WIDE)
     atoms_out = jnp.concatenate([jnp.where(mp == 0, keep, got), jnp.where(mp == 0, got, keep)])
     half = width // 2
     attn_local, mlp_local = attn_in.shape[2], mlp_up.shape[2]
@@ -859,16 +1058,30 @@
     up_sum = jnp.transpose(
         mlp_sum[: 4 * half].reshape(2, mlp_local // half, half, half), (2, 0, 1, 3)
     ).reshape(half, 2, mlp_local)
+    small, small_other = small.astype(WIDE), small_other.astype(WIDE)
+    small_pair = (
+        jnp.where(mp == 0, small, small_other),
+        jnp.where(mp == 0, small_other, small),
+    )
+    rows, part_rows = atom_width // 2, atom_width // 4
+    lanes = lax.dynamic_slice_in_dim(small[2 * rows :, :atom_width], section * rows, rows, 1)
+    cond_pair = [
+        jnp.where(mp == 0, cond_sum, cond_other).reshape(3, single, half),
+        jnp.where(mp == 0, cond_other, cond_sum).reshape(3, single, half),
+    ]
+    cond_total = jnp.transpose(jnp.concatenate(cond_pair, 2), (1, 0, 2))
     return (
         token_out.reshape(1, 1, batch, tokens, width),
         atoms_out.reshape(1, 1, batch, half_atoms, atom_width),
-        small[0].reshape(lanes)[:half_width],
-        small[1].reshape(half_width, 3, atom_width),
-        small[2].reshape(half_width, atom_width),
-        small[3].reshape(half_width, width),
-        jnp.transpose(cond_sum.reshape(1, 3, single, width), (0, 2, 1, 3)).astype(WIDE),
-        small[4].reshape(1, 3, width),
-        pair_out,
+        lanes[0],
+        jnp.concatenate([a[rows : rows + part_rows] for a in small_pair], 0).reshape(
+            rows, 3, atom_width
+        ),
+        jnp.concatenate([a[rows + part_rows : 2 * rows, :atom_width] for a in small_pair], 0),
+        jnp.concatenate([a[:rows] for a in small_pair], 1),
+        cond_total[None].astype(WIDE),
+        jnp.concatenate([a[2 * rows + 1 : 2 * rows + 4] for a in small_pair], 1)[None],
+        lanes[8:16].T,
         in_sum.astype(WIDE),
         attn_sum[4 * half :].astype(WIDE),
         up_sum.astype(WIDE),

time: 487 us -> 443 us (0.910)
  Pallas kernels: 157 us -> 334 us
  waiting for transfers between devices: 165 us -> 25.8 us
  starting transfers between devices: 54.3 us -> 9.67 us
  local copies, waits for them, and re-layouts: 66.7 us -> 45.1 us
  other arithmetic: 36.5 us -> 21.1 us
    pallas_call x3 -> x2, Pallas kernels: 73.7 us -> 251 us  [the longest x1 150 us: atom_back(): pl.pallas_call(atom_back_kernel, in_specs=everywhere(len(args)), out_spec...]
    ppermute x47 -> x11, waiting for transfers between devices: 165 us -> 25.8 us  [swap(): return lax.ppermute(array, axis, [(i, i ^ 1 << bit) for i in range(size)])]
    ppermute x47 -> x11, starting transfers between devices: 54.3 us -> 9.67 us  [swap(): return lax.ppermute(array, axis, [(i, i ^ 1 << bit) for i in range(size)])]
    unnamed x122 -> x83, local copies, waits for them, and re-layouts: 29.9 us -> 18.9 us
    convert_element_type x16 -> x1, other arithmetic: 11.6 us -> 2.09 us  [local(): cond_total[None].astype(WIDE)]
    reshape x8 -> x0, local copies, waits for them, and re-layouts: 5.48 us -> none  [the longest x1 1.64 us: local(): small[3].reshape(half_width, width)]
    select_n x17 -> x4, other arithmetic: 8.5 us -> 3.09 us  [both_halves(): jnp.where(me == 0, array, other)]
  transfers between devices with their start and end apart: 47 -> 11, of which waited for: 27 -> 3; matrix products, arithmetic and copies ran while one was open for 13% -> 5% of each run, Pallas kernels for 9% -> 10%
where the time goes in v2:
time: 443 us; the launch traced here: 437 us
  Pallas kernels  334 us (75%)
  local copies, waits for them, and re-layouts  45.1 us (10%)
  waiting for transfers between devices  25.8 us (6%)
  other arithmetic  21.1 us (5%)
  starting transfers between devices  9.67 us (2%)
    pallas_call x1, Pallas kernels, atom_back(): pl.pallas_call(atom_back_kernel, in_specs=everywhere(len(args)), out_spec...  150 us
    pallas_call x1, Pallas kernels, attention_back(): pl.pallas_call(attention_back_kernel, in_specs=everywhere(17), out_specs=...  101 us
    pallas_call x1, Pallas kernels, atom_front(): pl.pallas_call(atom_front_kernel, grid=(samples,), in_specs=[sample(count...  27.9 us
    ppermute x11, waiting for transfers between devices, swap(): return lax.ppermute(array, axis, [(i, i ^ 1 << bit) for i in range(size)])  25.8 us
    pallas_call x1, Pallas kernels, token_attention(): pl.pallas_call(token_attention_kernel, grid=(1,), in_specs=[whole(tokens....  20.1 us
    unnamed x83, local copies, waits for them, and re-layouts  18.9 us
    pallas_call x1, Pallas kernels, transition(): pl.pallas_call(transition_kernel, grid=(1,), in_specs=[whole(middle.shape...  18.8 us
    pallas_call x1, Pallas kernels, pair_bias(): pl.pallas_call(pair_kernel, grid=(tokens // block,), in_specs=[pl.BlockSp...  12.4 us
  transfers between devices with their start and end apart: 11, of which 3 were waited for; matrix products, arithmetic and copies ran while one was open for 5% of the time, Pallas kernels for 10%

profile of v2, /device:TPU:0, one launch (start us, length us, event | category | flops | bytes accessed | tf_op | source)
XLA Modules:
  0.0 437.2 jit_solution(3482646847508883573)
XLA Ops:
  0.7 1.9 constant_dynamic-slice_fusion.6
  2.5 3.0 collective-permute-start
  5.5 3.5 copy.81
  9.0 2.4 constant_dynamic-slice_fusion.5
  11.5 2.0 collective-permute-start.3
  13.5 1.7 constant_dynamic-slice_fusion.4
  15.2 2.0 collective-permute-start.2
  19.2 2.1 copy.82
  25.1 2.0 copy-done.6
  27.2 3.7 conditioning.1
  30.9 1.6 copy-done.12
  32.5 1.6 copy-done.13
  35.5 11.5 %collective-permute-done.2 = bf16[128,8]{0,1:T(8,128)(2,1)S(1)} collective-permute-done((bf16[128,8]{0,1:T(8,128)(2,1)S(1)}, bf16[128,8]{0,1:T(8,128)(2,1)S(1)}, u32[]{:S(2)}, u32[]{:S(2)}) %collective-permute-start.2) | collective-permute-done | bytes 2080 | tf_op jit(solution)/shard_map/ppermute | solution.py:936
  47.0 2.0 collective-permute-start.9
  49.0 2.9 copy-done.5
  51.9 12.4 %pair_bias.1 = (bf16[160,160,128]{2,1,0:T(8,128)(2,1)S(1)}, f32[16,160,160]{2,1,0:T(8,128)S(1)}) custom-call(bf16[160,160,128]{2,1,0:T(8,128)(2,1)S(1)} %copy-done.5, bf16[16,128]{1,0:T(8,128)(2,1)S(1)} %maximum_bitcast_fusion.4.weight_ref), custom_call_target="tpu_custom_call" | custom-call | flops 20000000000 | bytes 16000000 | tf_op jit(solution)/shard_map/pair_bias/pallas_call | solution.py:74
  64.3 2.7 copy-done.15
  67.2 1.9 broadcast_select_fusion.11
  69.1 14.3 %collective-permute-done.9 = bf16[384,768]{1,0:T(8,128)(2,1)S(1)} collective-permute-done((bf16[384,768]{1,0:T(8,128)(2,1)S(1)}, bf16[384,768]{1,0:T(8,128)(2,1)S(1)}, u32[]{:S(2)}, u32[]{:S(2)}) %collective-permute-start.9) | collective-permute-done | bytes 589856 | tf_op jit(solution)/shard_map/ppermute | solution.py:936
  83.9 27.9 %atom_front.1 = (bf16[2,1280,384]{2,1,0:T(8,128)(2,1)S(1)}, bf16[2,20,192,256]{3,2,1,0:T(8,128)(2,1)}, bf16[2,1280,128]{2,1,0:T(8,128)(2,1)S(1)}, bf16[2,160,768]{2,1,0:T(8,128)(2,1)S(1)}) custom-call(bf16[2,1280,128]{2,1,0:T(8,128)(2,1)S(1)} %pad_maximum_fusion.3.atoms_ref, bf16[1,128]{1,0:T(2,128)(2,1)S(1)} %bitcast.49, ...), custom_call_target="tpu_custom_call" | custom-call | flops 20000000000 | bytes 12000000 | tf_op jit(solution)/shard_map/atom_front/pallas_call | solution.py:226
  115.5 1.6 pad_maximum_fusion.in_b_ref
  117.1 1.6 broadcast_select_fusion.1
  118.7 1.6 pad_maximum_fusion.1.up_b_ref
  120.3 20.1 %token_attention.1 = (bf16[320,768]{1,0:T(8,128)(2,1)}, bf16[2,320,1152]{2,1,0:T(8,128)(2,1)}, f32[2,320,384]{2,1,0:T(8,128)}, f32[2,320,384]{2,1,0:T(8,128)}, b...) custom-call(bf16[320,768]{1,0:T(8,128)(2,1)} %bitcast.50, ...), custom_call_target="tpu_custom_call" | custom-call | flops 40000000000 | bytes 20000000 | tf_op jit(solution)/shard_map/token_attention/pallas_call | solution.py:312
  140.4 18.8 %transition.1 = (bf16[320,768]{1,0:T(8,128)(2,1)}, f32[320,768]{1,0:T(8,128)}, bf16[2,2,2304,384]{3,2,1,0:T(8,128)(2,1)}, bf16[2,1152,384]{2,1,0:T(8,128)(2,1)}, f32[3,1,768]{2,1,0:T(1,128)}) custom-call(f32[320,768]{1,0:T(8,128)} %get-tuple-element.51.middle_ref, f32[3,320,768]{2,1,0:T(8,128)} %copy-done.13, f32[3,320,768]{2,1,0:T(8,128)} %copy-done.13, ...), custom_call_target="tpu_custom_call" | custom-call | flops 60000002048 | bytes 20000000 | tf_op jit(solution)/shard_map/transition/pallas_call | solution.py:408
  159.2 100.6 %attention_back.1 = (bf16[320,768]{1,0:T(8,128)(2,1)}, bf16[2,2,3072,384]{3,2,1,0:T(8,128)(2,1)}, f32[3,1,768]{2,1,0:T(1,128)}, f32[16,160,160]{2,1,0:T(8,128)}, bf16[2304,384]{1,0:T(8,128)(2,1)}) custom-call(f32[320,768]{1,0:T(8,128)} %get-tuple-element.58.middle_grad_ref, bf16[320,768]{1,0:T(8,128)(2,1)} %bitcast.51, f32[3,320,768]{2,1,0:T(8,128)} %copy-done.12, ...), custom_call_target="tpu_custom_call" | custom-call | flops 60000002048 | bytes 24000000 | tf_op jit(solution)/shard_map/attention_back/pallas_call | solution.py:705
  259.8 150.3 %atom_back.1 = (f32[2,640,128]{2,1,0:T(8,128)}, bf16[2,640,128]{2,1,0:T(8,128)(2,1)}, bf16[320,768]{1,0:T(8,128)(2,1)}, bf16[1920,384]{1,0:T(8,128)(2,1)}, bf16[...) custom-call(bf16[2,1280,128]{2,1,0:T(8,128)(2,1)} %copy-done.2, ...), custom_call_target="tpu_custom_call" | custom-call | flops 60000002048 | bytes 24000000 | tf_op jit(solution)/shard_map/atom_back/pallas_call | solution.py:903
  414.4 1.8 slice_convert_fusion.1
  419.3 2.3 copy.85
  421.8 1.8 copy.77
  423.6 3.7 reshape.174
  430.4 2.1 convert_bitcast_fusion
  (149 shorter events, 26.4 us)
Async XLA Ops:
  0.6 23.7 %copy-start = (bf16[8,160,768]{2,1,0:T(8,128)(2,1)S(1)}, bf16[8,160,768]{2,1,0:T(8,128)(2,1)}, u32[]{:S(2)}) copy-start(bf16[8,160,768]{2,1,0:T(8,128)(2,1)} %param.37) | copy-start | bytes 5898244
  2.5 64.7 %collective-permute-start = (bf16[2,640,128]{2,1,0:T(8,128)(2,1)}, bf16[2,640,128]{2,1,0:T(8,128)(2,1)}, u32[]{:S(2)}, u32[]{:S(2)}) collective-permute-start(bf16[2,640,128]{2,1,0:T(8,128)(2,1)} %constant_dynamic-slice_fusion.6), channel_id=1, source_target_pairs={{0,8},{8,0},{1,9},{9,1},{2,10},{10,2},{3,11},{11,3},{4,12},{12,4},... | collective-permute-start | bytes 983048 | tf_op jit(solution)/shard_map/ppermute | solution.py:936
  5.5 29.2 %collective-permute-start.1 = (s32[20]{0:T(128)}, s32[20]{0:T(128)S(1)}, u32[]{:S(2)}, u32[]{:S(2)}) collective-permute-start(s32[20]{0:T(128)} %param.21), channel_id=1, source_target_pairs={{0,8},{8,0},{1,9},{9,1},{2,10},{10,2},{3,11},{11,3},{4,12},{12,4},... | collective-permute-start | bytes 248 | tf_op jit(solution)/shard_map/ppermute | solution.py:936
  9.0 6.2 %copy-start.36 = (bf16[128,8]{0,1:T(8,128)(2,1)S(1)}, bf16[128,8]{0,1:T(8,128)(2,1)}, u32[]{:S(2)}) copy-start(bf16[128,8]{0,1:T(8,128)(2,1)} %param.32) | copy-start | bytes 6148
  9.0 8.2 %copy-start.32 = (s32[1280]{0:T(1024)S(1)}, s32[1280]{0:T(1024)}, u32[]{:S(2)}) copy-start(s32[1280]{0:T(1024)} %param.20) | copy-start | bytes 15364
  9.0 9.5 %copy-start.31 = (bf16[128,3,128]{2,0,1:T(8,128)(2,1)S(1)}, bf16[128,3,128]{2,0,1:T(8,128)(2,1)}, u32[]{:S(2)}) copy-start(bf16[128,3,128]{2,0,1:T(8,128)(2,1)} %param.27) | copy-start | bytes 294916
  9.0 9.9 %copy-start.38 = (s32[8]{0:T(128)S(1)}, s32[8]{0:T(128)}, u32[]{:S(2)}) copy-start(s32[8]{0:T(128)} %param.22) | copy-start | bytes 100
  9.0 10.0 %copy-start.34 = (bf16[16,384]{1,0:T(8,128)(2,1)S(1)}, bf16[16,384]{1,0:T(8,128)(2,1)}, u32[]{:S(2)}) copy-start(bf16[16,384]{1,0:T(8,128)(2,1)} %param.23) | copy-start | bytes 36868
  9.0 10.1 %copy-start.35 = (bf16[2,3,768]{2,0,1:T(2,128)(2,1)S(1)}, bf16[2,3,768]{2,0,1:T(2,128)(2,1)}, u32[]{:S(2)}) copy-start(bf16[2,3,768]{2,0,1:T(2,128)(2,1)} %param.31) | copy-start | bytes 27652
  11.5 71.9 %collective-permute-start.3 = (bf16[384,1536]{1,0:T(8,128)(2,1)}, bf16[384,1536]{1,0:T(8,128)(2,1)S(1)}, u32[]{:S(2)}, u32[]{:S(2)}) collective-permute-start(bf16[384,1536]{1,0:T(8,128)(2,1)} %constant_dynamic-slice_fusion.5), channel_id=1, source_target_pairs={{0,8},{8,0},{1,9},{9,1},{2,10},{10,2},{3,11},{11,3},{4,12},{12,4},... | collective-permute-start | bytes 3538952 | tf_op jit(solution)/shard_map/ppermute | solution.py:936
  15.2 51.9 %collective-permute-start.5 = (bf16[192,768]{1,0:T(8,128)(2,1)}, bf16[192,768]{1,0:T(8,128)(2,1)}, u32[]{:S(2)}, u32[]{:S(2)}) collective-permute-start(bf16[192,768]{1,0:T(8,128)(2,1)} %constant_dynamic-slice_fusion.4), channel_id=1, source_target_pairs={{0,8},{8,0},{1,9},{9,1},{2,10},{10,2},{3,11},{11,3},{4,12},{12,4},... | collective-permute-start | bytes 884744 | tf_op jit(solution)/shard_map/ppermute | solution.py:936
  15.2 31.8 %collective-permute-start.2 = (bf16[128,8]{0,1:T(8,128)(2,1)S(1)}, bf16[128,8]{0,1:T(8,128)(2,1)S(1)}, u32[]{:S(2)}, u32[]{:S(2)}) collective-permute-start(bf16[128,8]{0,1:T(8,128)(2,1)S(1)} %copy-done.36), channel_id=1, source_target_pairs={{0,8},{8,0},{1,9},{9,1},{2,10},{10,2},{3,11},{11,3},{4,12},{12,4},... | collective-permute-start | bytes 6152 | tf_op jit(solution)/shard_map/ppermute | solution.py:936
  18.7 65.2 %copy-start.3 = (bf16[128,384]{1,0:T(8,128)(2,1)}, bf16[128,384]{1,0:T(8,128)(2,1)S(1)}, u32[]{:S(2)}) copy-start(bf16[128,384]{1,0:T(8,128)(2,1)S(1)} %copy.69.qkv_w_ref) | copy-start | bytes 294916
  18.9 65.1 %copy-start.4 = (f32[160,1]{1,0:T(8,128)}, f32[160,1]{1,0:T(8,128)S(1)}, u32[]{:S(2)}) copy-start(f32[160,1]{1,0:T(8,128)S(1)} %copy.70.inv_ref) | copy-start | bytes 1924
  21.3 3.8 copy-start.8
  27.1 7.6 %copy-start.37 = (s32[20]{0:T(128)S(1)}, s32[20]{0:T(128)}, u32[]{:S(2)}) copy-start(s32[20]{0:T(128)} %param.21) | copy-start | bytes 244
  27.2 19.9 %copy-start.24 = (bf16[384,768]{1,0:T(8,128)(2,1)S(1)}, bf16[384,768]{1,0:T(8,128)(2,1)}, u32[]{:S(2)}) copy-start(bf16[384,768]{1,0:T(8,128)(2,1)} %constant_dynamic-slice_fusion.1) | copy-start | bytes 1769476
  34.7 79.4 %collective-permute-start.7 = (bf16[384,1536]{1,0:T(8,128)(2,1)}, bf16[384,1536]{1,0:T(8,128)(2,1)}, u32[]{:S(2)}, u32[]{:S(2)}) collective-permute-start(bf16[384,1536]{1,0:T(8,128)(2,1)} %constant_dynamic-slice_fusion.2), channel_id=1, source_target_pairs={{0,8},{8,0},{1,9},{9,1},{2,10},{10,2},{3,11},{11,3},{4,12},{12,4},... | collective-permute-start | bytes 3538952 | tf_op jit(solution)/shard_map/ppermute | solution.py:936
  47.0 36.4 %collective-permute-start.9 = (bf16[384,768]{1,0:T(8,128)(2,1)S(1)}, bf16[384,768]{1,0:T(8,128)(2,1)S(1)}, u32[]{:S(2)}, u32[]{:S(2)}) collective-permute-start(bf16[384,768]{1,0:T(8,128)(2,1)S(1)} %copy-done.24), channel_id=1, source_target_pairs={{0,8},{8,0},{1,9},{9,1},{2,10},{10,2},{3,11},{11,3},{4,12},{12,4},... | collective-permute-start | bytes 1769480 | tf_op jit(solution)/shard_map/ppermute | solution.py:936
  67.1 16.8 %copy-start.16 = (f32[16,160,160]{2,1,0:T(8,128)}, f32[16,160,160]{2,1,0:T(8,128)S(1)}, u32[]{:S(2)}) copy-start(f32[16,160,160]{2,1,0:T(8,128)S(1)} %get-tuple-element.50.bias_ref) | copy-start | bytes 4915204
  67.1 16.8 %copy-start.7 = (bf16[128,768]{1,0:T(8,128)(2,1)S(1)}, bf16[128,768]{1,0:T(8,128)(2,1)}, u32[]{:S(2)}) copy-start(bf16[128,768]{1,0:T(8,128)(2,1)} %agg_w_ref.3) | copy-start | bytes 589828
  67.1 16.8 %copy-start.9 = (bf16[128,128]{1,0:T(8,128)(2,1)S(1)}, bf16[128,128]{1,0:T(8,128)(2,1)}, u32[]{:S(2)}) copy-start(bf16[128,128]{1,0:T(8,128)(2,1)} %out_w_ref.3) | copy-start | bytes 98308
  67.1 16.9 %copy-start.10 = (bf16[128]{0:T(256)(128)(2,1)S(1)}, bf16[128]{0:T(256)(128)(2,1)}, u32[]{:S(2)}) copy-start(bf16[128]{0:T(256)(128)(2,1)} %param.26) | copy-start | bytes 772
  67.1 44.8 %collective-permute-start.6 = (bf16[192,768]{1,0:T(8,128)(2,1)}, bf16[192,768]{1,0:T(8,128)(2,1)S(1)}, u32[]{:S(2)}, u32[]{:S(2)}) collective-permute-start(bf16[192,768]{1,0:T(8,128)(2,1)} %collective-permute-done.5), channel_id=1, source_target_pairs={{0,1},{1,0},{2,3},{3,2},{4,5},{5,4},{6,7},{7,6},{8,9},{9,8},{10,11... | collective-permute-start | bytes 884744 | tf_op jit(solution)/shard_map/ppermute | solution.py:936
  69.1 42.8 %copy-start.2 = (bf16[2,1280,128]{2,1,0:T(8,128)(2,1)}, bf16[2,1280,128]{2,1,0:T(8,128)(2,1)S(1)}, u32[]{:S(2)}) copy-start(bf16[2,1280,128]{2,1,0:T(8,128)(2,1)S(1)} %pad_maximum_fusion.3.atoms_ref) | copy-start | bytes 1966084
  83.4 30.7 %collective-permute-start.10 = (bf16[384,768]{1,0:T(8,128)(2,1)S(1)}, bf16[384,768]{1,0:T(8,128)(2,1)S(1)}, u32[]{:S(2)}, u32[]{:S(2)}) collective-permute-start(bf16[384,768]{1,0:T(8,128)(2,1)S(1)} %collective-permute-done.9), channel_id=1, source_target_pairs={{0,1},{1,0},{2,3},{3,2},{4,5},{5,4},{6,7},{7,6},{8,9},{9,8},{10,11... | collective-permute-start | bytes 1769480 | tf_op jit(solution)/shard_map/ppermute | solution.py:936
  83.4 31.9 %collective-permute-start.4 = (bf16[384,1536]{1,0:T(8,128)(2,1)S(1)}, bf16[384,1536]{1,0:T(8,128)(2,1)S(1)}, u32[]{:S(2)}, u32[]{:S(2)}) collective-permute-start(bf16[384,1536]{1,0:T(8,128)(2,1)S(1)} %collective-permute-done.3), channel_id=1, source_target_pairs={{0,1},{1,0},{2,3},{3,2},{4,5},{5,4},{6,7},{7,6},{8,9},{9,8},{10,11... | collective-permute-start | bytes 3538952 | tf_op jit(solution)/shard_map/ppermute | solution.py:936
  114.1 3.1 collective-permute-start.8
  411.1 6.4 %copy-start.20 = (bf16[2304,384]{1,0:T(8,128)(2,1)S(1)}, bf16[2304,384]{1,0:T(8,128)(2,1)}, u32[]{:S(2)}) copy-start(bf16[2304,384]{1,0:T(8,128)(2,1)} %get-tuple-element.82) | copy-start | bytes 5308420
  423.6 3.8 copy-start.25
  430.4 4.1 copy-start.23
  430.4 4.1 copy-start.27
  (18 other events, 44.8 us)
